TPU v7x, 32 devices: a whole 2x2x4 slice. The times are simulated.
32 devices in a mesh: pix: 16 (over z, y, x), frm: 2 (over core).
Axes of the slice: x: 2, y: 2, z: 4, core: 2. Of those that a mesh axis runs over, the one named last changes fastest.
Arguments:
- curves: bfloat16 [8192, 2048], P('pix', 'frm')
- annulus_of_block: int32 [32], P('pix'), may hold values from 0 to 3, as said below
- ref_blocks: int32 [4, 8], replicated, may hold values from 0 to 31, as said below
- keep_mask: int32 [32, 256], P('pix'), may hold values 0 or 1
- start_basis: bfloat16 [4, 32, 2048], P(None, None, 'frm'), may hold values from -6 to 6
Outputs:
- coefficients: float32 [32, 32, 256], P('pix')
Inputs may be any that keep to these rules, and one draw needn't show every extreme that they name: annulus_of_block names every annulus; block b + 16 has the annulus of block b. Every entry of ref_blocks[a, :] is a block of annulus a; each list names the lowest and the highest block of its annulus; entries may repeat.
All inputs are finite; a program needn't handle non-finite values. No bound on the sum of `keep_mask` on one device may be relied on, other than what follows from the above.
Results may differ from a plain program's by a relative error of at most 0.023.
Values may be sent and summed in bfloat16 or wider, within the bound.
No kernel may reach another device: no remote copies, remote signals or barrier semaphores. Data moves between devices by JAX's collectives and lax.ppermute only.
A program may use at most 64 MiB of HBM per device.

v0:
```python
import jax
import jax.numpy as jnp
from jax import lax
from jax.sharding import PartitionSpec as P

ITERS = 4


def shards(curves, annulus_of_block, ref_blocks, keep_mask, start_basis):
    nblocks = annulus_of_block.shape[0]
    frames = curves.shape[1]
    blocks = curves.reshape(nblocks, -1, frames)
    annuli = start_basis.shape[0]
    labels = jnp.arange(annuli, dtype=jnp.int32)
    member = annulus_of_block[:, None] == labels[None, :]
    selector = member.astype(jnp.bfloat16)
    member_f = member.astype(jnp.float32)
    global_ids = lax.axis_index("pix") * nblocks + jnp.arange(nblocks, dtype=jnp.int32)
    listed = jnp.any(
        (ref_blocks[None, :, :] == global_ids[:, None, None]) & member[:, :, None], axis=(1, 2)
    )
    weight = (listed[:, None] & (keep_mask == 1)).astype(jnp.float32)

    def project(basis_bf):
        chosen = jnp.einsum(
            "ba,akf->bkf", selector, basis_bf, preferred_element_type=jnp.float32
        ).astype(jnp.bfloat16)
        return jnp.einsum("bkf,bpf->bkp", chosen, blocks, preferred_element_type=jnp.float32)

    basis_bf = start_basis
    for step in range(ITERS):
        proj = (
            lax.psum(project(basis_bf).astype(jnp.bfloat16), "frm").astype(jnp.float32)
            * weight[:, None, :]
        )
        proj_bf = proj.astype(jnp.bfloat16)
        per_block = jnp.einsum("bkp,bpf->bkf", proj_bf, blocks, preferred_element_type=jnp.float32)
        local_span = jnp.einsum("ba,bkf->akf", member_f, per_block, precision=lax.Precision.HIGHEST)
        whole = lax.psum(local_span, "pix")
        inner = jnp.einsum("akf,ajf->akj", whole, whole, precision=lax.Precision.HIGHEST)
        gram = lax.psum(inner, "frm")
        lower = jnp.linalg.cholesky(gram)
        basis_bf = lax.linalg.triangular_solve(lower, whole, left_side=True, lower=True).astype(
            jnp.bfloat16
        )
    return lax.psum(project(basis_bf).astype(jnp.bfloat16), "frm").astype(jnp.float32)


def solution(mesh):
    in_specs = (P("pix", "frm"), P("pix"), P(), P("pix", None), P(None, None, "frm"))
    out_specs = P("pix", None, None)
    return jax.shard_map(shards, mesh=mesh, in_specs=in_specs, out_specs=out_specs, check_vma=False)
```

profile of v0, /device:TPU:0, one launch (start us, length us, event | category | flops | bytes accessed | tf_op | source)
XLA Modules:
  0.0 594.7 jit_solution(1470853487874488089)
XLA Ops:
  6.5 0.7 copy-done.5
  7.4 1.3 fusion.28
  8.7 0.4 convolution_convert_fusion.8
  9.1 3.8 psum.91
  13.0 0.2 and_reduce_fusion
  13.2 0.5 copy-done.7
  13.7 0.3 fusion.38
  14.0 1.7 fusion.18
  15.8 110.8 %all-reduce.5.cloned.1.call-done = f32[4,32,1024]{2,0,1:T(4,128)} async-done(((f32[4,32,1024]{2,0,1:T(4,128)}), f32[4,32,1024]{2,0,1:T(4,128)}) %all-reduce.5.cloned.1.call-update) | async-done | bytes 524304 | tf_op jit(solution)/shard_map/psum | solution.py:39
  126.5 2.4 fusion.10
  129.0 3.6 psum.93
  132.6 0.1 copy.25
  132.7 11.7 %custom-call.12 = f32[4,32,32]{2,1,0:T(8,128)S(1)} custom-call(f32[4,32,32]{2,1,0:T(8,128)S(1)} %fusion.37), custom_call_target="Cholesky" | custom-call | tf_op jit(solution)/shard_map/jit(cholesky)/cholesky | solution.py:42
  144.4 0.1 compare_reduce_fusion.3
  144.6 0.1 select_bitcast_fusion.3
  144.6 9.8 %custom-call.13 = f32[4,1,32,32]{2,3,1,0:T(8,128)S(1)} custom-call(f32[4,1,32,32]{3,2,1,0:T(8,128)S(1)} %select_bitcast_fusion.3), custom_call_target="InvertDiagBlocksLowerTriangular" | custom-call | tf_op jit(solution)/shard_map/triangular_solve/custom-call.0 | solution.py:43
  154.5 0.9 convolution_convert_fusion.3
  155.4 0.4 fusion.26
  155.8 0.4 convolution_convert_fusion.7
  156.2 3.6 psum.94
  159.8 0.3 fusion.39
  160.0 1.7 fusion.16
  161.8 107.4 %all-reduce.7.cloned.1.call-done = f32[4,32,1024]{2,0,1:T(4,128)} async-done(((f32[4,32,1024]{2,0,1:T(4,128)}), f32[4,32,1024]{2,0,1:T(4,128)}) %all-reduce.7.cloned.1.call-update) | async-done | bytes 524304 | tf_op jit(solution)/shard_map/psum | solution.py:39
  269.2 2.4 fusion.7
  271.6 3.6 psum.96
  275.2 0.1 copy.29
  275.3 11.7 %custom-call.14 = f32[4,32,32]{2,1,0:T(8,128)S(1)} custom-call(f32[4,32,32]{2,1,0:T(8,128)S(1)} %fusion.35), custom_call_target="Cholesky" | custom-call | tf_op jit(solution)/shard_map/jit(cholesky)/cholesky | solution.py:42
  287.0 0.1 compare_reduce_fusion.2
  287.2 0.1 select_bitcast_fusion.2
  287.3 9.8 %custom-call.15 = f32[4,1,32,32]{2,3,1,0:T(8,128)S(1)} custom-call(f32[4,1,32,32]{3,2,1,0:T(8,128)S(1)} %select_bitcast_fusion.2), custom_call_target="InvertDiagBlocksLowerTriangular" | custom-call | tf_op jit(solution)/shard_map/triangular_solve/custom-call.0 | solution.py:43
  297.1 0.9 convolution_convert_fusion.2
  298.0 0.4 fusion.24
  298.4 0.4 convolution_convert_fusion.6
  298.8 3.6 psum.97
  302.4 0.3 fusion.40
  302.7 1.7 fusion.14
  304.4 0.2 all-reduce.11.cloned.1.call-start
  304.6 107.2 %all-reduce.9.cloned.1.call-done = f32[4,32,1024]{2,0,1:T(4,128)} async-done(((f32[4,32,1024]{2,0,1:T(4,128)}), f32[4,32,1024]{2,0,1:T(4,128)}) %all-reduce.9.cloned.1.call-update) | async-done | bytes 524304 | tf_op jit(solution)/shard_map/psum | solution.py:39
  411.8 2.4 fusion.4
  414.2 3.6 psum.99
  417.8 0.1 copy.33
  417.9 11.7 %custom-call.16 = f32[4,32,32]{2,1,0:T(8,128)S(1)} custom-call(f32[4,32,32]{2,1,0:T(8,128)S(1)} %fusion.33), custom_call_target="Cholesky" | custom-call | tf_op jit(solution)/shard_map/jit(cholesky)/cholesky | solution.py:42
  429.7 0.1 compare_reduce_fusion.1
  429.8 0.1 select_bitcast_fusion.1
  429.9 9.8 %custom-call.17 = f32[4,1,32,32]{2,3,1,0:T(8,128)S(1)} custom-call(f32[4,1,32,32]{3,2,1,0:T(8,128)S(1)} %select_bitcast_fusion.1), custom_call_target="InvertDiagBlocksLowerTriangular" | custom-call | tf_op jit(solution)/shard_map/triangular_solve/custom-call.0 | solution.py:43
  439.7 0.9 convolution_convert_fusion.1
  440.6 0.4 fusion.22
  441.0 0.4 convolution_convert_fusion.5
  441.4 3.6 psum.100
  445.0 0.3 fusion.41
  445.3 1.7 fusion.12
  447.0 107.4 %all-reduce.11.cloned.1.call-done = f32[4,32,1024]{2,0,1:T(4,128)} async-done(((f32[4,32,1024]{2,0,1:T(4,128)}), f32[4,32,1024]{2,0,1:T(4,128)}) %all-reduce.11.cloned.1.call-update) | async-done | bytes 524304 | tf_op jit(solution)/shard_map/psum | solution.py:39
  554.4 2.4 fusion.1
  556.8 3.6 psum.102
  560.4 0.1 copy.37
  560.5 11.7 %custom-call.18 = f32[4,32,32]{2,1,0:T(8,128)S(1)} custom-call(f32[4,32,32]{2,1,0:T(8,128)S(1)} %fusion.31), custom_call_target="Cholesky" | custom-call | tf_op jit(solution)/shard_map/jit(cholesky)/cholesky | solution.py:42
  572.3 0.1 compare_reduce_fusion
  572.4 0.1 select_bitcast_fusion
  572.5 9.8 %custom-call.19 = f32[4,1,32,32]{2,3,1,0:T(8,128)S(1)} custom-call(f32[4,1,32,32]{3,2,1,0:T(8,128)S(1)} %select_bitcast_fusion), custom_call_target="InvertDiagBlocksLowerTriangular" | custom-call | tf_op jit(solution)/shard_map/triangular_solve/custom-call.0 | solution.py:43
  582.3 0.9 convolution_convert_fusion
  583.2 0.4 fusion.20
  583.6 0.4 convolution_convert_fusion.4
  584.0 3.6 psum.103
  587.6 0.6 convert_element_type.97
  (34 shorter events, 0.5 us)
Async XLA Ops:
  6.5 2.1 copy-start
  6.5 120.0 %all-reduce.5.cloned.1.call-start = ((), (), s32[]{:S(2)}) async-start(), calls=%async_computation | async-start | bytes 1048576 | tf_op jit(solution)/shard_map/psum | solution.py:39
  6.5 0.7 copy-start.5
  9.1 3.8 copy-start.6
  12.9 0.7 copy-start.7
  15.7 253.5 %all-reduce.7.cloned.1.call-start = ((), (), s32[]{:S(2)}) async-start(), calls=%async_computation.1 | async-start | bytes 1048576 | tf_op jit(solution)/shard_map/psum | solution.py:39
  126.5 27.9 %copy-start.1 = (f32[4,32,1024]{2,0,1:T(4,128)S(1)}, f32[4,32,1024]{2,0,1:T(4,128)}, u32[]{:S(2)}) copy-start(f32[4,32,1024]{2,0,1:T(4,128)} %all-reduce.5.cloned.1.call-done) | copy-start | bytes 1572868
  161.7 250.0 %all-reduce.9.cloned.1.call-start = ((), (), s32[]{:S(2)}) async-start(), calls=%async_computation.2 | async-start | bytes 1048576 | tf_op jit(solution)/shard_map/psum | solution.py:39
  269.2 27.9 %copy-start.2 = (f32[4,32,1024]{2,0,1:T(4,128)S(1)}, f32[4,32,1024]{2,0,1:T(4,128)}, u32[]{:S(2)}) copy-start(f32[4,32,1024]{2,0,1:T(4,128)} %all-reduce.7.cloned.1.call-done) | copy-start | bytes 1572868
  304.4 250.0 %all-reduce.11.cloned.1.call-start = ((), (), s32[]{:S(2)}) async-start(), calls=%async_computation.3 | async-start | bytes 1048576 | tf_op jit(solution)/shard_map/psum | solution.py:39
  411.8 27.9 %copy-start.3 = (f32[4,32,1024]{2,0,1:T(4,128)S(1)}, f32[4,32,1024]{2,0,1:T(4,128)}, u32[]{:S(2)}) copy-start(f32[4,32,1024]{2,0,1:T(4,128)} %all-reduce.9.cloned.1.call-done) | copy-start | bytes 1572868
  554.4 27.9 %copy-start.4 = (f32[4,32,1024]{2,0,1:T(4,128)S(1)}, f32[4,32,1024]{2,0,1:T(4,128)}, u32[]{:S(2)}) copy-start(f32[4,32,1024]{2,0,1:T(4,128)} %all-reduce.11.cloned.1.call-done) | copy-start | bytes 1572868
Sparse Core Ops, SparseCore 0:
  15.8 110.6 all-reduce.4
  161.9 107.2 all-reduce.6
  304.5 107.2 all-reduce.8
  447.1 107.2 all-reduce.10
where the time goes:
time: 595 us
  waiting for transfers between devices  433 us (73%)
  other arithmetic  88.3 us (15%)
  blocking collectives  32.5 us (5%)
  matrix products  25.9 us (4%)
  between operations  13.4 us (2%)
    psum x4, waiting for transfers between devices, shards(): whole = lax.psum(local_span, 'pix')  433 us
    another operation x13, other arithmetic, shards(): lower = jnp.linalg.cholesky(gram)  47.5 us
    another operation x9, other arithmetic, shards(): lax.linalg.triangular_solve(lower, whole, left_side=True, lower=True)  39.7 us
    psum x5, blocking collectives, shards(): lax.psum(project(basis_bf).astype(jnp.bfloat16), 'frm').astype(jnp.float32)  18.1 us
    psum x4, blocking collectives, shards(): gram = lax.psum(inner, 'frm')  14.3 us
  transfers between devices with their start and end apart: 4, of which 4 were waited for; matrix products, arithmetic and copies ran while one was open for 0% of the time, Pallas kernels for 0%

commit v1 on v0

v1 whole, which is shorter than its diff:
```python
import functools

import jax
import jax.numpy as jnp
from jax import lax
from jax.experimental import pallas as pl
from jax.experimental.pallas import tpu as pltpu
from jax.sharding import PartitionSpec as P

ITERS = 4
LANES = 128
BOTH = ("pix", "frm")
EXACT = lax.Precision.HIGHEST


def inverse_factor(gram):
    k = gram.shape[0]
    rows = lax.broadcasted_iota(jnp.int32, (k, LANES), 0)
    cols = lax.broadcasted_iota(jnp.int32, (k, LANES), 1)
    wide = jnp.concatenate([gram, jnp.zeros((k, LANES - k), jnp.float32)], axis=1)
    wide = wide + jnp.where(cols == rows + k, 1.0, 0.0)
    for step in range(k - 1):
        pivot_row = wide[step : step + 1, :]
        scaled = pivot_row / pivot_row[:, step : step + 1]
        factor = jnp.where(rows > step, jnp.broadcast_to(wide[:, step : step + 1], (k, LANES)), 0.0)
        wide = wide - factor * scaled
    pivots = jnp.sum(jnp.where(cols == rows, wide, 0.0), axis=1, keepdims=True)
    return wide[:, k : 2 * k] * lax.rsqrt(pivots)


def load_curves(frm, own_ref, got_refs, held, sems):
    chunk, frames = held.shape
    width = own_ref.shape[1]
    others = len(got_refs) + 1
    copies = [
        pltpu.make_async_copy(
            own_ref.at[pl.ds(frm * chunk, chunk)],
            held.at[:, pl.ds(pl.multiple_of(frm * width, LANES), width)],
            sems.at[0],
        )
    ]
    for shift, got in enumerate(got_refs, 1):
        source = lax.rem(frm - shift + others, others)
        copies.append(
            pltpu.make_async_copy(
                got.at[pl.ds(0, chunk)],
                held.at[:, pl.ds(pl.multiple_of(source * width, LANES), width)],
                sems.at[shift],
            )
        )
    for copy in copies:
        copy.start()
    return copies


def project(basis, held):
    return lax.dot_general(
        basis, held[...], (((1,), (1,)), ((), ())), preferred_element_type=jnp.float32
    )


def store_span(proj, weight, held, out_ref):
    proj_bf = (proj * weight).astype(jnp.bfloat16)
    span = jnp.dot(proj_bf, held[...], preferred_element_type=jnp.float32)
    parts, rows = out_ref.shape[0], 32 * held.shape[1] // LANES // out_ref.shape[0]
    across = held.shape[1] // LANES
    for j in range(parts):
        top, left = j // across * rows, j % across * LANES
        out_ref[j, :rows, :] = span[top : top + rows, left : left + LANES].astype(out_ref.dtype)


def first_kernel(others, pos_ref, ann_ref, own_ref, start_ref, weight_ref, *refs):
    got_refs, (out_ref, held, basis, sems) = refs[: others - 1], refs[others - 1 :]
    frm, label = pos_ref[0], ann_ref[0]
    chunk = held.shape[0]
    width = own_ref.shape[1]
    copies = load_curves(frm, own_ref, got_refs, held, sems)
    copies.append(
        pltpu.make_async_copy(
            start_ref.at[label],
            basis.at[:, pl.ds(pl.multiple_of(frm * width, LANES), width)],
            sems.at[others],
        )
    )
    copies[-1].start()
    for shift, got in enumerate(got_refs, 1):
        source = lax.rem(frm - shift + others, others)
        copies.append(
            pltpu.make_async_copy(
                got.at[pl.ds(chunk, basis.shape[0])],
                basis.at[:, pl.ds(pl.multiple_of(source * width, LANES), width)],
                sems.at[others + shift],
            )
        )
        copies[-1].start()
    rows = out_ref.shape[1] - 8
    mark = jnp.full((8, LANES), label, jnp.int32).astype(jnp.float32)
    for j in range(out_ref.shape[0]):
        out_ref[j, rows:, :] = mark
    for copy in copies:
        copy.wait()
    store_span(project(basis[...], held), weight_ref[...], held, out_ref)


def step_kernel(others, last, pos_ref, span_ref, own_ref, weight_ref, *refs):
    got_refs, (out_ref, held, whole, sems) = refs[: others - 1], refs[others - 1 :]
    copies = load_curves(pos_ref[0], own_ref, got_refs, held, sems)
    parts, rows = span_ref.shape[:2]
    across = held.shape[1] // LANES
    for j in range(parts):
        top, left = j // across * rows, j % across * LANES
        whole[top : top + rows, left : left + LANES] = span_ref[j].astype(jnp.float32)
    span = whole[...]
    gram = lax.dot_general(
        span, span, (((1,), (1,)), ((), ())), precision=EXACT, preferred_element_type=jnp.float32
    )
    ortho = jnp.dot(
        inverse_factor(gram), span, precision=EXACT, preferred_element_type=jnp.float32
    )
    basis = ortho.astype(jnp.bfloat16)
    for copy in copies:
        copy.wait()
    proj = project(basis, held)
    if last:
        out_ref[...] = proj
    else:
        store_span(proj, weight_ref[...], held, out_ref)


def sum_kernel(annuli, first, in_ref, *refs):
    parts, rows = in_ref.shape[0], refs[0].shape[1]
    if first:
        out_ref, mark_ref = refs
        for j in range(parts):
            mark_ref[j : j + 1, :] = in_ref[j, rows : rows + 1, :]
    else:
        mark_ref, out_ref = refs
        rows = out_ref.shape[1]

    def add(j, sums):
        part = in_ref[j, :rows, :].astype(jnp.float32)
        mark = mark_ref[pl.ds(j, 1), :]
        return tuple(s + jnp.where(mark == a, part, 0.0) for a, s in enumerate(sums))

    def give(j, sums):
        mark = mark_ref[pl.ds(j, 1), :]
        total = sums[0]
        for a in range(1, annuli):
            total = jnp.where(mark == a, sums[a], total)
        out_ref[j] = total.astype(out_ref.dtype)

    sums = tuple(jnp.zeros((rows, LANES), jnp.float32) for _ in range(annuli))
    if parts <= 32:
        for j in range(parts):
            sums = add(j, sums)
        for j in range(parts):
            give(j, sums)
    else:
        sums = lax.fori_loop(0, parts, add, sums)
        lax.fori_loop(0, parts, lambda j, c: (give(j, sums), c)[1], 0)


def shards(npix, nfrm, curves, annulus_of_block, ref_blocks, keep_mask, start_basis):
    pixels, width = curves.shape
    nblocks, block = keep_mask.shape
    annuli, comps, _ = start_basis.shape
    chunk, frames, parts = pixels // nfrm, width * nfrm, npix * nfrm
    rows = comps * frames // LANES // parts
    pix, frm = lax.axis_index("pix"), lax.axis_index("frm")

    def label_at(place):
        return annulus_of_block[place * chunk // block]

    got = []
    for shift in range(1, nfrm):
        target = lax.rem(frm + shift, nfrm)
        message = jnp.concatenate(
            [
                lax.dynamic_slice_in_dim(curves, target * chunk, chunk, 0),
                lax.dynamic_index_in_dim(start_basis, label_at(target), 0, keepdims=False),
            ]
        )
        got.append(lax.ppermute(message, "frm", [(i, (i + shift) % nfrm) for i in range(nfrm)]))

    label = label_at(frm)
    mine = pix * nblocks + frm * chunk // block
    listed = jnp.any(lax.dynamic_index_in_dim(ref_blocks, label, 0) == mine)
    kept = lax.dynamic_slice_in_dim(keep_mask.reshape(1, pixels), frm * chunk, chunk, 1)
    weight = (listed & (kept == 1)).astype(jnp.float32)
    position = frm.reshape(1)

    smem = pl.BlockSpec(memory_space=pltpu.SMEM)
    vmem = pl.BlockSpec(memory_space=pltpu.VMEM)
    anyw = pl.BlockSpec(memory_space=pl.ANY)
    shape = jax.ShapeDtypeStruct
    held = pltpu.VMEM((chunk, frames), jnp.bfloat16)
    params = pltpu.CompilerParams(vmem_limit_bytes=32 * 1024 * 1024)

    sent = pl.pallas_call(
        functools.partial(first_kernel, nfrm),
        out_shape=shape((parts, rows + 8, LANES), jnp.float32),
        in_specs=[smem, smem, anyw, anyw, vmem] + [anyw] * (nfrm - 1),
        out_specs=vmem,
        scratch_shapes=[
            held,
            pltpu.VMEM((comps, frames), jnp.bfloat16),
            pltpu.SemaphoreType.DMA((2 * nfrm,)),
        ],
        compiler_params=params,
        name="first_span",
    )(position, label.reshape(1), curves, start_basis, weight, *got)

    marks = None
    for step in range(ITERS):
        kind = jnp.float32
        taken = lax.all_to_all(sent, BOTH, 0, 0, tiled=True)
        total_shape = shape((parts, rows, LANES), kind)
        if step == 0:
            total, marks = pl.pallas_call(
                functools.partial(sum_kernel, annuli, True),
                out_shape=(total_shape, shape((parts, LANES), jnp.float32)),
                in_specs=[vmem],
                out_specs=(vmem, vmem),
                compiler_params=params,
                name="sum_first",
            )(taken)
        else:
            total = pl.pallas_call(
                functools.partial(sum_kernel, annuli, False),
                out_shape=total_shape,
                in_specs=[vmem, vmem],
                out_specs=vmem,
                compiler_params=params,
                name="sum_spans",
            )(taken, marks)
        span = lax.all_to_all(total, BOTH, 0, 0, tiled=True)
        last = step == ITERS - 1
        sent = pl.pallas_call(
            functools.partial(step_kernel, nfrm, last),
            out_shape=shape((comps, chunk) if last else (parts, rows, LANES), jnp.float32),
            in_specs=[smem, vmem, anyw, vmem] + [anyw] * (nfrm - 1),
            out_specs=vmem,
            scratch_shapes=[
                held,
                pltpu.VMEM((comps, frames), jnp.float32),
                pltpu.SemaphoreType.DMA((nfrm,)),
            ],
            compiler_params=params,
            name="fit" if last else "step",
        )(position, span, curves, weight, *got)

    if nfrm == 2 and chunk == block:
        other = lax.ppermute(sent, "frm", [(0, 1), (1, 0)])
        low, high = jnp.where(frm == 0, sent, other), jnp.where(frm == 0, other, sent)
        return jnp.stack([low, high])
    every = lax.all_gather(sent, "frm")
    return every.swapaxes(0, 1).reshape(comps, nblocks, block).swapaxes(0, 1)


def solution(mesh):
    in_specs = (P("pix", "frm"), P("pix"), P(), P("pix", None), P(None, None, "frm"))
    out_specs = P("pix", None, None)
    body = functools.partial(shards, mesh.shape["pix"], mesh.shape["frm"])
    return jax.shard_map(body, mesh=mesh, in_specs=in_specs, out_specs=out_specs, check_vma=False)
```

time: 595 us -> 142 us (0.24)
  waiting for transfers between devices: 433 us -> 1.19 us
  other arithmetic: 88.3 us -> 2.79 us
  blocking collectives: 32.5 us -> 110 us
  matrix products: 25.9 us -> 0 us
  Pallas kernels: 0 us -> 20.9 us
  between operations: 13.4 us -> 3.93 us
    psum x4 -> x0, waiting for transfers between devices: 433 us -> none  [shards(): whole = lax.psum(local_span, 'pix')]
    all_to_all x0 -> x8, blocking collectives: none -> 110 us  [the longest x4 58.4 us: shards(): taken = lax.all_to_all(sent, BOTH, 0, 0, tiled=True)]
    another operation x22 -> x2, other arithmetic: 87.2 us -> 0.64 us  [shards(): return jnp.stack([low, high])]
    psum x9 -> x0, blocking collectives: 32.5 us -> none  [the longest x5 18.1 us: shards(): lax.psum(project(basis_bf).astype(jnp.bfloat16), 'frm').astype(jnp.float32)]
    dot_general x22 -> x0, matrix products: 22.3 us -> none  [the longest x4 9.71 us: shards(): jnp.einsum('akf,ajf->akj', whole, whole, precision=lax.Precision.HIGHEST)]
    pallas_call x0 -> x9, Pallas kernels: none -> 20.9 us  [the longest x4 18.4 us: shards(): pl.pallas_call(functools.partial(step_kernel, nfrm, last), out_shape=shap...]
  transfers between devices with their start and end apart: 4 -> 2, of which waited for: 4 -> 1; matrix products, arithmetic and copies ran while one was open for 0% -> 1% of each run, Pallas kernels for 0% -> 0%
where the time goes in v1:
time: 142 us
  blocking collectives  110 us (77%)
  Pallas kernels  20.9 us (15%)
  between operations  3.93 us (3%)
  other arithmetic  2.79 us (2%)
  local copies, waits for them, and re-layouts  2.6 us (2%)
    all_to_all x4, blocking collectives, shards(): taken = lax.all_to_all(sent, BOTH, 0, 0, tiled=True)  58.4 us
    all_to_all x4, blocking collectives, shards(): span = lax.all_to_all(total, BOTH, 0, 0, tiled=True)  51.5 us
    pallas_call x4, Pallas kernels, shards(): pl.pallas_call(functools.partial(step_kernel, nfrm, last), out_shape=shap...  18.4 us
  transfers between devices with their start and end apart: 2, of which 1 were waited for; matrix products, arithmetic and copies ran while one was open for 1% of the time, Pallas kernels for 0%

profile of v1, /device:TPU:0, one launch (start us, length us, event | category | flops | bytes accessed | tf_op | source)
XLA Modules:
  0.0 141.8 jit_solution(8996458546491181035)
XLA Ops:
  0.0 0.0 copy-start.1
  0.0 1.4 fusion
  2.8 0.0 copy-start.2
  2.8 0.0 copy-start
  2.8 1.2 constant_dynamic-slice_fusion
  4.7 0.0 copy-done.1
  4.8 0.5 collective-permute-start
  6.4 0.0 copy-done.2
  7.0 1.4 compare_reduce_fusion
  8.4 0.7 and_convert_fusion.weight_ref
  9.1 0.0 collective-permute-done.refs_0_
  9.1 0.0 copy-done
  9.1 1.6 %first_span.1 = f32[32,24,128]{2,1,0:T(8,128)S(1)} custom-call(s32[1]{0:T(128)} %bitcast.pos_ref, s32[1]{0:T(128)} %get-tuple-element.12.ann_ref, bf16[512,1024]{1,0:T(8,128)(2,1)S(1)} %copy-done, bf16[4,32,1024]{2,1,0:T(8,128)(2,1)S(1)} %copy-done.1, f32[1,256]{1,0:T(1,128)S(1)} %and_convert_fusion.weight_ref, ...), custom_call_target="tpu_custom_call" | custom-call | tf_op jit(solution)/shard_map/first_span/pallas_call | solution.py:199
  10.7 19.9 %all_to_all.40.in_ref = f32[32,24,128]{2,1,0:T(8,128)S(1)} all-to-all(f32[32,24,128]{2,1,0:T(8,128)S(1)} %first_span.1), channel_id=1, replica_groups=mesh['pix'=16,'frm'=2] {'pix','frm'}, dimensions={0} | all-to-all | bytes 786432 | tf_op jit(solution)/shard_map/all_to_all | solution.py:216
  30.7 0.2 sum_first.1
  30.9 13.0 %all_to_all.41.span_ref = f32[32,16,128]{2,1,0:T(8,128)S(1)} all-to-all(f32[32,16,128]{2,1,0:T(8,128)S(1)} %get-tuple-element.7), channel_id=1, replica_groups=mesh['pix'=16,'frm'=2] {'pix','frm'}, dimensions={0} | all-to-all | bytes 524288 | tf_op jit(solution)/shard_map/all_to_all | solution.py:236
  44.0 4.7 %step.3 = f32[32,16,128]{2,1,0:T(8,128)S(1)} custom-call(s32[1]{0:T(128)} %bitcast.pos_ref, f32[32,16,128]{2,1,0:T(8,128)S(1)} %all_to_all.41.span_ref, bf16[512,1024]{1,0:T(8,128)(2,1)S(1)} %copy-done, f32[1,256]{1,0:T(1,128)S(1)} %and_convert_fusion.weight_ref, bf16[288,1024]{1,0:T(8,128)(2,1)S(1)} %collective-permute-done.refs_0_), custom_call_target="tpu_custom_call" | custom-call | tf_op jit(solution)/shard_map/step/pallas_call | solution.py:238
  48.7 12.8 %all_to_all.42.in_ref = f32[32,16,128]{2,1,0:T(8,128)S(1)} all-to-all(f32[32,16,128]{2,1,0:T(8,128)S(1)} %step.3), channel_id=1, replica_groups=mesh['pix'=16,'frm'=2] {'pix','frm'}, dimensions={0} | all-to-all | bytes 524288 | tf_op jit(solution)/shard_map/all_to_all | solution.py:216
  61.5 0.2 sum_spans.3
  61.7 12.8 %all_to_all.43.span_ref = f32[32,16,128]{2,1,0:T(8,128)S(1)} all-to-all(f32[32,16,128]{2,1,0:T(8,128)S(1)} %sum_spans.3), channel_id=1, replica_groups=mesh['pix'=16,'frm'=2] {'pix','frm'}, dimensions={0} | all-to-all | bytes 524288 | tf_op jit(solution)/shard_map/all_to_all | solution.py:236
  74.5 4.7 %step.4 = f32[32,16,128]{2,1,0:T(8,128)S(1)} custom-call(s32[1]{0:T(128)} %bitcast.pos_ref, f32[32,16,128]{2,1,0:T(8,128)S(1)} %all_to_all.43.span_ref, bf16[512,1024]{1,0:T(8,128)(2,1)S(1)} %copy-done, f32[1,256]{1,0:T(1,128)S(1)} %and_convert_fusion.weight_ref, bf16[288,1024]{1,0:T(8,128)(2,1)S(1)} %collective-permute-done.refs_0_), custom_call_target="tpu_custom_call" | custom-call | tf_op jit(solution)/shard_map/step/pallas_call | solution.py:238
  79.2 12.8 %all_to_all.44.in_ref = f32[32,16,128]{2,1,0:T(8,128)S(1)} all-to-all(f32[32,16,128]{2,1,0:T(8,128)S(1)} %step.4), channel_id=1, replica_groups=mesh['pix'=16,'frm'=2] {'pix','frm'}, dimensions={0} | all-to-all | bytes 524288 | tf_op jit(solution)/shard_map/all_to_all | solution.py:216
  92.1 0.2 sum_spans.4
  92.3 12.8 %all_to_all.45.span_ref = f32[32,16,128]{2,1,0:T(8,128)S(1)} all-to-all(f32[32,16,128]{2,1,0:T(8,128)S(1)} %sum_spans.4), channel_id=1, replica_groups=mesh['pix'=16,'frm'=2] {'pix','frm'}, dimensions={0} | all-to-all | bytes 524288 | tf_op jit(solution)/shard_map/all_to_all | solution.py:236
  105.1 4.7 %step.5 = f32[32,16,128]{2,1,0:T(8,128)S(1)} custom-call(s32[1]{0:T(128)} %bitcast.pos_ref, f32[32,16,128]{2,1,0:T(8,128)S(1)} %all_to_all.45.span_ref, bf16[512,1024]{1,0:T(8,128)(2,1)S(1)} %copy-done, f32[1,256]{1,0:T(1,128)S(1)} %and_convert_fusion.weight_ref, bf16[288,1024]{1,0:T(8,128)(2,1)S(1)} %collective-permute-done.refs_0_), custom_call_target="tpu_custom_call" | custom-call | tf_op jit(solution)/shard_map/step/pallas_call | solution.py:238
  109.8 12.8 %all_to_all.46.in_ref = f32[32,16,128]{2,1,0:T(8,128)S(1)} all-to-all(f32[32,16,128]{2,1,0:T(8,128)S(1)} %step.5), channel_id=1, replica_groups=mesh['pix'=16,'frm'=2] {'pix','frm'}, dimensions={0} | all-to-all | bytes 524288 | tf_op jit(solution)/shard_map/all_to_all | solution.py:216
  122.6 0.2 sum_spans.5
  122.8 12.8 %all_to_all.47.span_ref = f32[32,16,128]{2,1,0:T(8,128)S(1)} all-to-all(f32[32,16,128]{2,1,0:T(8,128)S(1)} %sum_spans.5), channel_id=1, replica_groups=mesh['pix'=16,'frm'=2] {'pix','frm'}, dimensions={0} | all-to-all | bytes 524288 | tf_op jit(solution)/shard_map/all_to_all | solution.py:236
  135.6 4.2 %fit.1 = f32[32,256]{1,0:T(8,128)S(1)} custom-call(s32[1]{0:T(128)} %bitcast.pos_ref, f32[32,16,128]{2,1,0:T(8,128)S(1)} %all_to_all.47.span_ref, bf16[512,1024]{1,0:T(8,128)(2,1)S(1)} %copy-done, f32[1,256]{1,0:T(1,128)S(1)} %and_convert_fusion.weight_ref, bf16[288,1024]{1,0:T(8,128)(2,1)S(1)} %collective-permute-done.refs_0_), custom_call_target="tpu_custom_call" | custom-call | tf_op jit(solution)/shard_map/fit/pallas_call | solution.py:238
  139.9 0.1 collective-permute-start.1
  140.0 1.2 collective-permute-done.1
  141.2 0.6 pad_maximum_fusion.1
  (4 shorter events, 0.1 us)
Async XLA Ops:
  0.0 4.7 %copy-start.1 = (bf16[4,32,1024]{2,1,0:T(8,128)(2,1)S(1)}, bf16[4,32,1024]{2,1,0:T(8,128)(2,1)}, u32[]{:S(2)}) copy-start(bf16[4,32,1024]{2,1,0:T(8,128)(2,1)} %start_ref.1) | copy-start | bytes 786436
  2.8 3.6 %copy-start.2 = (s32[2,256]{1,0:T(2,128)S(1)}, s32[2,256]{1,0:T(2,128)}, u32[]{:S(2)}) copy-start(s32[2,256]{1,0:T(2,128)} %param.8) | copy-start | bytes 6148
  2.8 6.3 %copy-start = (bf16[512,1024]{1,0:T(8,128)(2,1)S(1)}, bf16[512,1024]{1,0:T(8,128)(2,1)}, u32[]{:S(2)}) copy-start(bf16[512,1024]{1,0:T(8,128)(2,1)} %own_ref.9) | copy-start | bytes 3145732
  4.8 4.3 %collective-permute-start = (bf16[288,1024]{1,0:T(8,128)(2,1)S(1)}, bf16[288,1024]{1,0:T(8,128)(2,1)S(1)}, u32[]{:S(2)}, u32[]{:S(2)}) collective-permute-start(bf16[288,1024]{1,0:T(8,128)(2,1)S(1)} %pad_maximum_fusion), channel_id=1, source_target_pairs={{0,1},{1,0},{2,3},{3,2},{4,5},{5,4},{6,7},{7,6},{8,9},{9,8},{10,11... | collective-permute-start | bytes 1769480 | tf_op jit(solution)/shard_map/ppermute | solution.py:183
  139.9 1.3 collective-permute-start.1

commit v2 on v0

v2 whole, which is shorter than its diff:
```python
import functools

import jax
import jax.numpy as jnp
from jax import lax
from jax.experimental import pallas as pl
from jax.experimental.pallas import tpu as pltpu
from jax.sharding import PartitionSpec as P

ITERS = 4
LANES = 128
PANEL = 16
BOTH = ("pix", "frm")
EXACT = lax.Precision.HIGHEST
ROWS_TO_ROWS = (((1,), (1,)), ((), ()))


def inverse_factor(gram):
    k = gram.shape[0]
    rows = lax.broadcasted_iota(jnp.int32, (k, LANES), 0)
    cols = lax.broadcasted_iota(jnp.int32, (k, LANES), 1)
    wide = jnp.concatenate([gram, jnp.zeros((k, LANES - k), jnp.float32)], axis=1)
    wide = wide + jnp.where(cols == rows + k, 1.0, 0.0)
    for base in range(0, k, PANEL):
        low, below = wide[base:, :], rows[base:, :]
        panel = [jnp.broadcast_to(low[:, base + j : base + j + 1], low.shape) for j in range(PANEL)]
        for j in range(PANEL):
            factor = jnp.where(below > base + j, panel[j] * (1.0 / panel[j][j : j + 1, :]), 0.0)
            for i in range(j + 1, PANEL):
                panel[i] = panel[i] - factor * panel[i][j : j + 1, :]
            low = low - factor * low[j : j + 1, :]
        wide = jnp.concatenate([wide[:base, :], low], axis=0) if base else low
    pivots = jnp.sum(jnp.where(cols == rows, wide, 0.0), axis=1, keepdims=True)
    return wide[:, k : 2 * k] * lax.rsqrt(pivots)


def pieces(wide):
    high = wide.astype(jnp.bfloat16)
    rest = wide - high.astype(jnp.float32)
    middle = rest.astype(jnp.bfloat16)
    low = (rest - middle.astype(jnp.float32)).astype(jnp.bfloat16)
    return jnp.concatenate([high, middle, low], axis=0)


def fold(stacked, k):
    return (stacked[2 * k :] + stacked[k : 2 * k]) + stacked[:k]


def dot_rows(left, right):
    return lax.dot_general(left, right, ROWS_TO_ROWS, preferred_element_type=jnp.float32)


def tiles(parts, rows, across):
    for j in range(parts):
        yield j, pl.ds(j // across * rows, rows), pl.ds(j % across * LANES, LANES)


def store_span(span, out_ref):
    parts, rows = out_ref.shape[:2]
    for j, down, along in tiles(parts, rows, span.shape[1] // LANES):
        out_ref[j] = lax.slice(
            span, (down.start, along.start), (down.start + rows, along.start + LANES)
        ).astype(out_ref.dtype)


def wait_all(copies):
    for copy in copies:
        copy.start()
    for copy in copies:
        copy.wait()


def pack_kernel(chunk, block, others, ann_ref, own_ref, start_ref, *refs):
    out_refs, sems = refs[:-1], refs[-1]
    frm = lax.axis_index("frm")
    copies = []
    for shift, out_ref in enumerate(out_refs, 1):
        target = lax.rem(frm + shift, others)
        label = ann_ref[target * chunk // block]
        copies += [
            pltpu.make_async_copy(
                own_ref.at[pl.ds(pl.multiple_of(target * chunk, chunk), chunk)],
                out_ref.at[pl.ds(0, chunk)],
                sems.at[2 * shift - 2],
            ),
            pltpu.make_async_copy(
                start_ref.at[label],
                out_ref.at[pl.ds(chunk, start_ref.shape[1])],
                sems.at[2 * shift - 1],
            ),
        ]
    wait_all(copies)


def first_kernel(block, others, ann_ref, listed_ref, keep_ref, own_ref, start_ref, *refs):
    got_refs = refs[: others - 1]
    out_ref, held, weight_ref, basis, sems = refs[others - 1 :]
    pix, frm = lax.axis_index("pix"), lax.axis_index("frm")
    chunk, width = held.shape[0], own_ref.shape[1]
    place = frm * chunk // block
    label = ann_ref[place]
    copies = []
    for shift in range(others):
        source = lax.rem(frm - shift + others, others)
        along = pl.ds(pl.multiple_of(source * width, LANES), width)
        if shift:
            curves = got_refs[shift - 1].at[pl.ds(0, chunk)]
            start = got_refs[shift - 1].at[pl.ds(chunk, basis.shape[0])]
        else:
            curves = own_ref.at[pl.ds(pl.multiple_of(frm * chunk, chunk), chunk)]
            start = start_ref.at[label]
        copies += [
            pltpu.make_async_copy(curves, held.at[:, along], sems.at[2 * shift]),
            pltpu.make_async_copy(start, basis.at[:, along], sems.at[2 * shift + 1]),
        ]
    for copy in copies:
        copy.start()
    mine = pix * ann_ref.shape[0] + place
    listed = listed_ref[label, 0] == mine
    for entry in range(1, listed_ref.shape[1]):
        listed = listed | (listed_ref[label, entry] == mine)
    listed = listed.astype(jnp.int32)
    kept = keep_ref[pl.ds(frm, 1), :]
    weight = jnp.where(kept == 1, listed, 0).astype(jnp.float32)
    weight_ref[...] = weight
    for copy in copies:
        copy.wait()
    proj_bf = (dot_rows(basis[...], held[...]) * weight).astype(jnp.bfloat16)
    span = jnp.dot(proj_bf, held[...], preferred_element_type=jnp.float32)
    store_span(span + ((1 - listed) * label).astype(jnp.float32), out_ref)


def step_kernel(last, span_ref, held, weight_ref, out_ref, whole):
    parts, rows = span_ref.shape[:2]
    for j, down, along in tiles(parts, rows, held.shape[1] // LANES):
        whole[down, along] = span_ref[j]
    span = whole[...]
    comps = span.shape[0]
    if span.dtype == jnp.bfloat16:
        gram = dot_rows(span, span)
        raw = dot_rows(span, held[...])
    else:
        gram = lax.dot_general(
            span, span, ROWS_TO_ROWS, precision=EXACT, preferred_element_type=jnp.float32
        )
        raw = fold(dot_rows(pieces(span), held[...]), comps)
    proj = jnp.dot(inverse_factor(gram), raw, precision=EXACT, preferred_element_type=jnp.float32)
    if last:
        out_ref[...] = proj
    else:
        proj_bf = (proj * weight_ref[...]).astype(jnp.bfloat16)
        store_span(jnp.dot(proj_bf, held[...], preferred_element_type=jnp.float32), out_ref)


def add_and_give(annuli, in_ref, mark_ref, give_ref, out_ref):
    parts, rows = out_ref.shape[:2]

    def add(j, sums):
        part = in_ref[j].astype(jnp.float32)
        mark = mark_ref[pl.ds(j, 1), :]
        return tuple(s + jnp.where(mark == a, part, 0.0) for a, s in enumerate(sums))

    def give(j, sums):
        mark = give_ref[pl.ds(j, 1), :]
        total = sums[0]
        for a in range(1, annuli):
            total = jnp.where(mark == a, sums[a], total)
        out_ref[j] = total.astype(out_ref.dtype)
        return sums

    sums = tuple(jnp.zeros((rows, LANES), jnp.float32) for _ in range(annuli))
    if parts <= 32:
        for j in range(parts):
            sums = add(j, sums)
        for j in range(parts):
            give(j, sums)
    else:
        sums = lax.fori_loop(0, parts, add, sums)
        lax.fori_loop(0, parts, give, sums)


def first_sum_kernel(annuli, chunks, listed_ref, in_ref, out_ref, give_ref, mark_ref, table):
    parts = in_ref.shape[0]
    blocks = table.shape[0]
    for b in range(blocks):
        table[b] = -1
    for a in range(annuli):
        for entry in range(listed_ref.shape[1]):
            table[listed_ref[a, entry]] = a
    for j in range(parts):
        label = jnp.full((1, LANES), table[j // chunks], jnp.int32)
        said = in_ref[j, :1, :].astype(jnp.int32)
        mark_ref[j : j + 1, :] = label
        give_ref[j : j + 1, :] = jnp.where(label < 0, said, label)
    add_and_give(annuli, in_ref, mark_ref, give_ref, out_ref)


def sum_kernel(annuli, in_ref, give_ref, out_ref):
    add_and_give(annuli, in_ref, give_ref, give_ref, out_ref)


def shards(npix, nfrm, curves, annulus_of_block, ref_blocks, keep_mask, start_basis):
    pixels, width = curves.shape
    nblocks, block = keep_mask.shape
    annuli, comps, _ = start_basis.shape
    chunk, frames, parts = pixels // nfrm, width * nfrm, npix * nfrm
    rows = comps * frames // LANES // parts
    narrow = jnp.bfloat16 if rows % 16 == 0 else jnp.float32

    smem = pl.BlockSpec(memory_space=pltpu.SMEM)
    vmem = pl.BlockSpec(memory_space=pltpu.VMEM)
    anyw = pl.BlockSpec(memory_space=pl.ANY)
    shape = jax.ShapeDtypeStruct

    def call(kernel, out, ins, outs, name, scratch=()):
        return pl.pallas_call(
            kernel,
            out_shape=out,
            in_specs=ins,
            out_specs=outs,
            scratch_shapes=list(scratch),
            compiler_params=pltpu.CompilerParams(vmem_limit_bytes=32 * 1024 * 1024),
            name=name,
        )

    messages = call(
        functools.partial(pack_kernel, chunk, block, nfrm),
        [shape((chunk + comps, width), jnp.bfloat16)] * (nfrm - 1),
        [smem, anyw, anyw],
        [vmem] * (nfrm - 1),
        "pack",
        [pltpu.SemaphoreType.DMA((2 * nfrm - 2,))],
    )(annulus_of_block, curves, start_basis)
    got = [
        lax.ppermute(message, "frm", [(i, (i + shift) % nfrm) for i in range(nfrm)])
        for shift, message in enumerate(messages, 1)
    ]
    sent, held, weight = call(
        functools.partial(first_kernel, block, nfrm),
        (
            shape((parts, rows, LANES), jnp.float32),
            shape((chunk, frames), jnp.bfloat16),
            shape((1, chunk), jnp.float32),
        ),
        [smem, smem, vmem] + [anyw] * (nfrm + 1),
        (vmem, vmem, vmem),
        "first_span",
        [pltpu.VMEM((comps, frames), jnp.bfloat16), pltpu.SemaphoreType.DMA((2 * nfrm,))],
    )(annulus_of_block, ref_blocks, keep_mask.reshape(nfrm, chunk), curves, start_basis, *got)

    give = None
    for step in range(ITERS):
        kind = narrow if step else jnp.float32
        taken = lax.all_to_all(sent, BOTH, 0, 0, tiled=True)
        total = shape((parts, rows, LANES), kind)
        if step == 0:
            total, give = call(
                functools.partial(first_sum_kernel, annuli, parts // (npix * nblocks)),
                (total, shape((parts, LANES), jnp.int32)),
                [smem, vmem],
                (vmem, vmem),
                "first_sum",
                [
                    pltpu.VMEM((parts, LANES), jnp.int32),
                    pltpu.SMEM((npix * nblocks,), jnp.int32),
                ],
            )(ref_blocks, taken)
        else:
            total = call(
                functools.partial(sum_kernel, annuli), total, [vmem, vmem], vmem, "sum"
            )(taken, give)
        span = lax.all_to_all(total, BOTH, 0, 0, tiled=True)
        last = step == ITERS - 1
        sent = call(
            functools.partial(step_kernel, last),
            shape((comps, chunk), jnp.float32) if last else shape((parts, rows, LANES), narrow),
            [vmem, vmem, vmem],
            vmem,
            "fit" if last else "step",
            [pltpu.VMEM((comps, frames), kind)],
        )(span, held, weight)

    if nfrm == 2 and chunk == block:
        frm = lax.axis_index("frm")
        other = lax.ppermute(sent, "frm", [(0, 1), (1, 0)])
        return jnp.stack([jnp.where(frm == 0, sent, other), jnp.where(frm == 0, other, sent)])
    every = lax.all_gather(sent, "frm")
    return every.swapaxes(0, 1).reshape(comps, nblocks, block).swapaxes(0, 1)


def solution(mesh):
    in_specs = (P("pix", "frm"), P("pix"), P(), P("pix", None), P(None, None, "frm"))
    out_specs = P("pix", None, None)
    body = functools.partial(shards, mesh.shape["pix"], mesh.shape["frm"])
    return jax.shard_map(body, mesh=mesh, in_specs=in_specs, out_specs=out_specs, check_vma=False)
```

time: 595 us -> 108 us (0.18)
  waiting for transfers between devices: 433 us -> 2.62 us
  other arithmetic: 88.3 us -> 0.64 us
  blocking collectives: 32.5 us -> 90.9 us
  matrix products: 25.9 us -> 0 us
  between operations: 13.4 us -> 0.05 us
  Pallas kernels: 0 us -> 9.62 us
    psum x4 -> x0, waiting for transfers between devices: 433 us -> none  [shards(): whole = lax.psum(local_span, 'pix')]
    all_to_all x0 -> x8, blocking collectives: none -> 90.9 us  [the longest x4 48.1 us: shards(): taken = lax.all_to_all(sent, BOTH, 0, 0, tiled=True)]
    another operation x22 -> x2, other arithmetic: 87.2 us -> 0.64 us  [shards(): jnp.stack([jnp.where(frm == 0, sent, other), jnp.where(frm == 0, other, s...]
    psum x9 -> x0, blocking collectives: 32.5 us -> none  [the longest x5 18.1 us: shards(): lax.psum(project(basis_bf).astype(jnp.bfloat16), 'frm').astype(jnp.float32)]
    dot_general x22 -> x0, matrix products: 22.3 us -> none  [the longest x4 9.71 us: shards(): jnp.einsum('akf,ajf->akj', whole, whole, precision=lax.Precision.HIGHEST)]
    pallas_call x0 -> x10, Pallas kernels: none -> 9.62 us  [the longest x4 5.76 us: shards(): call(functools.partial(step_kernel, last), shape((comps, chunk), jnp.floa...]
  transfers between devices with their start and end apart: 4 -> 2, of which waited for: 4 -> 2; matrix products, arithmetic and copies ran while one was open for 0% -> 0% of each run, Pallas kernels for 0% -> 0%
where the time goes in v2:
time: 108 us; the launch traced here: 107 us
  blocking collectives  90.9 us (84%)
  Pallas kernels  9.62 us (9%)
  local copies, waits for them, and re-layouts  2.84 us (3%)
  waiting for transfers between devices  2.62 us (2%)
    all_to_all x4, blocking collectives, shards(): taken = lax.all_to_all(sent, BOTH, 0, 0, tiled=True)  48.1 us
    all_to_all x4, blocking collectives, shards(): span = lax.all_to_all(total, BOTH, 0, 0, tiled=True)  42.8 us
    pallas_call x4, Pallas kernels, shards(): call(functools.partial(step_kernel, last), shape((comps, chunk), jnp.floa...  5.76 us
    unnamed x10, local copies, waits for them, and re-layouts  2.84 us
  transfers between devices with their start and end apart: 2, of which 2 were waited for; matrix products, arithmetic and copies ran while one was open for 0% of the time, Pallas kernels for 0%

profile of v2, /device:TPU:0, one launch (start us, length us, event | category | flops | bytes accessed | tf_op | source)
XLA Modules:
  0.0 107.4 jit_solution(13682836621369245070)
XLA Ops:
  0.0 0.0 copy-start
  0.0 1.2 %copy-done = bf16[512,1024]{1,0:T(8,128)(2,1)S(1)} copy-done((bf16[512,1024]{1,0:T(8,128)(2,1)S(1)}, bf16[512,1024]{1,0:T(8,128)(2,1)}, u32[]{:S(2)}) %copy-start) | copy-done | bytes 1048600
  1.2 0.0 copy-start.1
  1.2 0.9 copy-done.1
  2.2 0.0 copy-start.3
  2.2 0.7 copy-done.3
  2.8 0.0 copy-start.2
  2.8 0.0 copy-start.4
  2.8 0.7 pack.1
  3.5 0.5 collective-permute-start
  4.1 1.6 %collective-permute-done.refs_0_ = bf16[288,1024]{1,0:T(8,128)(2,1)S(1)} collective-permute-done((bf16[288,1024]{1,0:T(8,128)(2,1)S(1)}, bf16[288,1024]{1,0:T(8,128)(2,1)S(1)}, u32[]{:S(2)}, u32[]{:S(2)}) %collective-permute-start) | collective-permute-done | bytes 589856 | tf_op jit(solution)/shard_map/ppermute | solution.py:235
  5.7 0.0 copy-done.2
  5.7 0.0 copy-done.4
  5.7 1.6 %first_span.1 = (f32[32,16,128]{2,1,0:T(8,128)S(1)}, bf16[256,2048]{1,0:T(8,128)(2,1)S(1)}, f32[1,256]{1,0:T(1,128)S(1)}) custom-call(s32[2]{0:T(128)S(1)} %copy-done.3, s32[4,8]{1,0:T(4,128)S(1)} %copy-done.2, s32[2,256]{1,0:T(2,128)S(1)} %copy-done.4, bf16[512,1024]{1,0:T(8,128)(2,1)S(1)} %copy-done, bf16[4,32,1024]{2,1,0:T(8,128)(2,1)S(1)} %copy-done.1, ...), custom_call_target="tpu_custom_call" | custom-call | tf_op jit(solution)/shard_map/first_span/pallas_call | solution.py:238
  7.3 17.6 %all_to_all.40.in_ref = f32[32,16,128]{2,1,0:T(8,128)S(1)} all-to-all(f32[32,16,128]{2,1,0:T(8,128)S(1)} %get-tuple-element.10), channel_id=1, replica_groups=mesh['pix'=16,'frm'=2] {'pix','frm'}, dimensions={0} | all-to-all | bytes 524288 | tf_op jit(solution)/shard_map/all_to_all | solution.py:254
  25.0 0.8 first_sum.1
  25.8 12.8 %all_to_all.41.span_ref = f32[32,16,128]{2,1,0:T(8,128)S(1)} all-to-all(f32[32,16,128]{2,1,0:T(8,128)S(1)} %get-tuple-element.11), channel_id=1, replica_groups=mesh['pix'=16,'frm'=2] {'pix','frm'}, dimensions={0} | all-to-all | bytes 524288 | tf_op jit(solution)/shard_map/all_to_all | solution.py:272
  38.6 1.7 %step.3 = bf16[32,16,128]{2,1,0:T(8,128)(2,1)S(1)} custom-call(f32[32,16,128]{2,1,0:T(8,128)S(1)} %all_to_all.41.span_ref, bf16[256,2048]{1,0:T(8,128)(2,1)S(1)} %get-tuple-element.12.held, f32[1,256]{1,0:T(1,128)S(1)} %get-tuple-element.13.weight_ref), custom_call_target="tpu_custom_call" | custom-call | tf_op jit(solution)/shard_map/step/pallas_call | solution.py:274
  40.3 10.4 %all_to_all.42.in_ref = bf16[32,16,128]{2,1,0:T(8,128)(2,1)S(1)} all-to-all(bf16[32,16,128]{2,1,0:T(8,128)(2,1)S(1)} %step.3), channel_id=1, replica_groups=mesh['pix'=16,'frm'=2] {'pix','frm'}, dimensions={0} | all-to-all | bytes 262144 | tf_op jit(solution)/shard_map/all_to_all | solution.py:254
  50.8 0.2 sum.3
  51.0 10.0 %all_to_all.43.span_ref = bf16[32,16,128]{2,1,0:T(8,128)(2,1)S(1)} all-to-all(bf16[32,16,128]{2,1,0:T(8,128)(2,1)S(1)} %sum.3), channel_id=1, replica_groups=mesh['pix'=16,'frm'=2] {'pix','frm'}, dimensions={0} | all-to-all | bytes 262144 | tf_op jit(solution)/shard_map/all_to_all | solution.py:272
  61.0 1.5 %step.4 = bf16[32,16,128]{2,1,0:T(8,128)(2,1)S(1)} custom-call(bf16[32,16,128]{2,1,0:T(8,128)(2,1)S(1)} %all_to_all.43.span_ref, bf16[256,2048]{1,0:T(8,128)(2,1)S(1)} %get-tuple-element.12.held, f32[1,256]{1,0:T(1,128)S(1)} %get-tuple-element.13.weight_ref), custom_call_target="tpu_custom_call" | custom-call | tf_op jit(solution)/shard_map/step/pallas_call | solution.py:274
  62.5 10.0 %all_to_all.44.in_ref = bf16[32,16,128]{2,1,0:T(8,128)(2,1)S(1)} all-to-all(bf16[32,16,128]{2,1,0:T(8,128)(2,1)S(1)} %step.4), channel_id=1, replica_groups=mesh['pix'=16,'frm'=2] {'pix','frm'}, dimensions={0} | all-to-all | bytes 262144 | tf_op jit(solution)/shard_map/all_to_all | solution.py:254
  72.5 0.2 sum.4
  72.7 10.0 %all_to_all.45.span_ref = bf16[32,16,128]{2,1,0:T(8,128)(2,1)S(1)} all-to-all(bf16[32,16,128]{2,1,0:T(8,128)(2,1)S(1)} %sum.4), channel_id=1, replica_groups=mesh['pix'=16,'frm'=2] {'pix','frm'}, dimensions={0} | all-to-all | bytes 262144 | tf_op jit(solution)/shard_map/all_to_all | solution.py:272
  82.7 1.5 %step.5 = bf16[32,16,128]{2,1,0:T(8,128)(2,1)S(1)} custom-call(bf16[32,16,128]{2,1,0:T(8,128)(2,1)S(1)} %all_to_all.45.span_ref, bf16[256,2048]{1,0:T(8,128)(2,1)S(1)} %get-tuple-element.12.held, f32[1,256]{1,0:T(1,128)S(1)} %get-tuple-element.13.weight_ref), custom_call_target="tpu_custom_call" | custom-call | tf_op jit(solution)/shard_map/step/pallas_call | solution.py:274
  84.2 10.0 %all_to_all.46.in_ref = bf16[32,16,128]{2,1,0:T(8,128)(2,1)S(1)} all-to-all(bf16[32,16,128]{2,1,0:T(8,128)(2,1)S(1)} %step.5), channel_id=1, replica_groups=mesh['pix'=16,'frm'=2] {'pix','frm'}, dimensions={0} | all-to-all | bytes 262144 | tf_op jit(solution)/shard_map/all_to_all | solution.py:254
  94.2 0.2 sum.5
  94.4 10.0 %all_to_all.47.span_ref = bf16[32,16,128]{2,1,0:T(8,128)(2,1)S(1)} all-to-all(bf16[32,16,128]{2,1,0:T(8,128)(2,1)S(1)} %sum.5), channel_id=1, replica_groups=mesh['pix'=16,'frm'=2] {'pix','frm'}, dimensions={0} | all-to-all | bytes 262144 | tf_op jit(solution)/shard_map/all_to_all | solution.py:272
  104.4 1.1 %fit.1 = f32[32,256]{1,0:T(8,128)S(1)} custom-call(bf16[32,16,128]{2,1,0:T(8,128)(2,1)S(1)} %all_to_all.47.span_ref, bf16[256,2048]{1,0:T(8,128)(2,1)S(1)} %get-tuple-element.12.held, f32[1,256]{1,0:T(1,128)S(1)} %get-tuple-element.13.weight_ref), custom_call_target="tpu_custom_call" | custom-call | tf_op jit(solution)/shard_map/fit/pallas_call | solution.py:274
  105.6 0.2 collective-permute-start.1
  105.8 1.0 collective-permute-done.1
  106.8 0.6 pad_maximum_fusion
  (1 shorter events, 0.0 us)
Async XLA Ops:
  0.0 1.2 %copy-start = (bf16[512,1024]{1,0:T(8,128)(2,1)S(1)}, bf16[512,1024]{1,0:T(8,128)(2,1)}, u32[]{:S(2)}) copy-start(bf16[512,1024]{1,0:T(8,128)(2,1)} %own_ref.3) | copy-start | bytes 3145732
  1.2 0.9 copy-start.1
  2.2 0.7 copy-start.3
  2.8 2.9 %copy-start.2 = (s32[4,8]{1,0:T(4,128)S(1)}, s32[4,8]{1,0:T(4,128)}, u32[]{:S(2)}) copy-start(s32[4,8]{1,0:T(4,128)} %listed_ref.3) | copy-start | bytes 388
  2.8 2.9 %copy-start.4 = (s32[2,256]{1,0:T(2,128)S(1)}, s32[2,256]{1,0:T(2,128)}, u32[]{:S(2)}) copy-start(s32[2,256]{1,0:T(2,128)} %keep_ref.1) | copy-start | bytes 6148
  3.5 2.1 %collective-permute-start = (bf16[288,1024]{1,0:T(8,128)(2,1)S(1)}, bf16[288,1024]{1,0:T(8,128)(2,1)S(1)}, u32[]{:S(2)}, u32[]{:S(2)}) collective-permute-start(bf16[288,1024]{1,0:T(8,128)(2,1)S(1)} %pack.1), channel_id=1, source_target_pairs={{0,1},{1,0},{2,3},{3,2},{4,5},{5,4},{6,7},{7,6},{8,9},{9,8},{10,11... | collective-permute-start | bytes 1769480 | tf_op jit(solution)/shard_map/ppermute | solution.py:235
  105.6 1.2 %collective-permute-start.1 = (f32[32,256]{1,0:T(8,128)S(1)}, f32[32,256]{1,0:T(8,128)S(1)}, u32[]{:S(2)}, u32[]{:S(2)}) collective-permute-start(f32[32,256]{1,0:T(8,128)S(1)} %fit.1), channel_id=1, source_target_pairs={{0,1},{1,0},{2,3},{3,2},{4,5},{5,4},{6,7},{7,6},{8,9},{9,8},{10,11... | collective-permute-start | bytes 98312 | tf_op jit(solution)/shard_map/ppermute | solution.py:285

commit v3 on v2

v3 whole, which is shorter than its diff:
```python
import functools

import jax
import jax.numpy as jnp
from jax import lax
from jax.experimental import pallas as pl
from jax.experimental.pallas import tpu as pltpu
from jax.sharding import PartitionSpec as P

ITERS = 4
LANES = 128
PANEL = 16
BOTH = ("pix", "frm")
EXACT = lax.Precision.HIGHEST
ROWS_TO_ROWS = (((1,), (1,)), ((), ()))


def inverse_factor(gram):
    k = gram.shape[0]
    rows = lax.broadcasted_iota(jnp.int32, (k, LANES), 0)
    cols = lax.broadcasted_iota(jnp.int32, (k, LANES), 1)
    wide = jnp.concatenate([gram, jnp.zeros((k, LANES - k), jnp.float32)], axis=1)
    wide = wide + jnp.where(cols == rows + k, 1.0, 0.0)
    for base in range(0, k, PANEL):
        low, below = wide[base:, :], rows[base:, :]
        panel = [jnp.broadcast_to(low[:, base + j : base + j + 1], low.shape) for j in range(PANEL)]
        for j in range(PANEL):
            factor = jnp.where(below > base + j, panel[j] * (1.0 / panel[j][j : j + 1, :]), 0.0)
            for i in range(j + 1, PANEL):
                panel[i] = panel[i] - factor * panel[i][j : j + 1, :]
            low = low - factor * low[j : j + 1, :]
        wide = jnp.concatenate([wide[:base, :], low], axis=0) if base else low
    pivots = jnp.sum(jnp.where(cols == rows, wide, 0.0), axis=1, keepdims=True)
    return wide[:, k : 2 * k] * lax.rsqrt(pivots)


def pieces(wide):
    high = wide.astype(jnp.bfloat16)
    rest = wide - high.astype(jnp.float32)
    middle = rest.astype(jnp.bfloat16)
    low = (rest - middle.astype(jnp.float32)).astype(jnp.bfloat16)
    return jnp.concatenate([high, middle, low], axis=0)


def fold(stacked, k):
    return (stacked[2 * k :] + stacked[k : 2 * k]) + stacked[:k]


def dot_rows(left, right):
    return lax.dot_general(left, right, ROWS_TO_ROWS, preferred_element_type=jnp.float32)


def store_tiles(span, first, across, out_ref):
    rows = out_ref.shape[1]
    for down in range(span.shape[0] // rows):
        for along in range(span.shape[1] // LANES):
            tile = span[down * rows : (down + 1) * rows, along * LANES : (along + 1) * LANES]
            out_ref[first + (down * across + along)] = tile.astype(out_ref.dtype)


def span_of(proj, weight, held, sources, out_ref):
    proj_bf = (proj * weight).astype(jnp.bfloat16)
    width = held[0].shape[1] // LANES
    for curves, source in zip(held, sources):
        span = jnp.dot(proj_bf, curves[...], preferred_element_type=jnp.float32)
        yield span, source * width, width * len(held)


def frame_order(others):
    frm = lax.axis_index("frm")
    return [lax.rem(frm - shift + others, others) for shift in range(others)]


def pack_kernel(own_ref, *refs):
    out_refs, sems = refs[:-1], refs[-1]
    others = len(out_refs) + 1
    chunk = out_refs[0].shape[0]
    copies = []
    for shift, out_ref in enumerate(out_refs, 1):
        target = lax.rem(lax.axis_index("frm") + shift, others)
        rows = pl.ds(pl.multiple_of(target * chunk, chunk), chunk)
        copies.append(pltpu.make_async_copy(own_ref.at[rows], out_ref, sems.at[shift - 1]))
    for copy in copies:
        copy.start()
    for copy in copies:
        copy.wait()


def own_kernel(
    block, chunks, ann_ref, listed_ref, keep_ref, all_ref, start_ref,
    own_ref, raw_ref, weight_ref, say_ref, mark_ref, basis, table, sems,
):
    pix, frm = lax.axis_index("pix"), lax.axis_index("frm")
    chunk = own_ref.shape[0]
    rows = pl.ds(pl.multiple_of(frm * chunk, chunk), chunk)
    place = frm * chunk // block
    label = ann_ref[place]
    curves = pltpu.make_async_copy(all_ref.at[rows], own_ref, sems.at[0])
    start = pltpu.make_async_copy(start_ref.at[label], basis, sems.at[1])
    curves.start()
    start.start()
    for b in range(table.shape[0]):
        table[b] = -1
    for a in range(listed_ref.shape[0]):
        for entry in range(listed_ref.shape[1]):
            table[listed_ref[a, entry]] = a
    for j in range(mark_ref.shape[0]):
        mark_ref[j : j + 1, :] = jnp.full((1, LANES), table[j // chunks], jnp.int32)
    listed = (table[pix * ann_ref.shape[0] + place] >= 0).astype(jnp.int32)
    kept = keep_ref[pl.ds(frm, 1), :]
    weight_ref[...] = jnp.where(kept == 1, listed, 0).astype(jnp.float32)
    say_ref[...] = jnp.full((1, LANES), (1 - listed) * label, jnp.int32).astype(jnp.float32)
    curves.wait()
    start.wait()
    raw_ref[...] = dot_rows(basis[...], own_ref[...])


def first_kernel(block, others, ann_ref, raw_ref, weight_ref, say_ref, own_ref, *refs):
    got, starts, out_ref = refs[: others - 1], refs[others - 1 : -1], refs[-1]
    label = ann_ref[lax.axis_index("frm") * own_ref.shape[0] // block]
    proj = raw_ref[...]
    for curves, start in zip(got, starts):
        proj = proj + dot_rows(start[label], curves[...])
    held, weight = (own_ref, *got), weight_ref[...]
    for span, first, across in span_of(proj, weight, held, frame_order(others), out_ref):
        store_tiles(
            jnp.concatenate(
                [
                    span[:, i : i + LANES] + say_ref[...]
                    for i in range(0, span.shape[1], LANES)
                ],
                axis=1,
            ),
            first,
            across,
            out_ref,
        )


def step_kernel(last, others, span_ref, weight_ref, *refs):
    held, (out_ref, whole) = refs[:others], refs[others:]
    parts, rows = span_ref.shape[:2]
    comps, frames = whole.shape
    across, width = frames // LANES, frames // others
    for j in range(parts):
        down, along = j // across * rows, j % across * LANES
        whole[down : down + rows, along : along + LANES] = span_ref[j]
    span, sources = whole[...], frame_order(others)
    raw = jnp.zeros((comps, held[0].shape[0]), jnp.float32)
    for curves, source in zip(held, sources):
        part = whole[:, pl.ds(pl.multiple_of(source * width, LANES), width)]
        if span.dtype == jnp.bfloat16:
            raw = raw + dot_rows(part, curves[...])
        else:
            raw = raw + fold(dot_rows(pieces(part), curves[...]), comps)
    if span.dtype == jnp.bfloat16:
        gram = dot_rows(span, span)
    else:
        gram = lax.dot_general(
            span, span, ROWS_TO_ROWS, precision=EXACT, preferred_element_type=jnp.float32
        )
    proj = jnp.dot(inverse_factor(gram), raw, precision=EXACT, preferred_element_type=jnp.float32)
    if last:
        out_ref[...] = proj
    else:
        for span, first, across in span_of(proj, weight_ref[...], held, sources, out_ref):
            store_tiles(span, first, across, out_ref)


def place_kernel(own_ref, other_ref, out_ref, sems):
    frm = lax.axis_index("frm")
    copies = [
        pltpu.make_async_copy(own_ref, out_ref.at[frm], sems.at[0]),
        pltpu.make_async_copy(other_ref, out_ref.at[1 - frm], sems.at[1]),
    ]
    for copy in copies:
        copy.start()
    for copy in copies:
        copy.wait()


def add_and_give(annuli, in_ref, mark_ref, give_ref, out_ref):
    parts, rows = out_ref.shape[:2]

    def add(j, sums):
        part = in_ref[j].astype(jnp.float32)
        mark = mark_ref[pl.ds(j, 1), :]
        return tuple(s + jnp.where(mark == a, part, 0.0) for a, s in enumerate(sums))

    def give(j, sums):
        mark = give_ref[pl.ds(j, 1), :]
        total = sums[0]
        for a in range(1, annuli):
            total = jnp.where(mark == a, sums[a], total)
        out_ref[j] = total.astype(out_ref.dtype)
        return sums

    sums = tuple(jnp.zeros((rows, LANES), jnp.float32) for _ in range(annuli))
    if parts <= 32:
        for j in range(parts):
            sums = add(j, sums)
        for j in range(parts):
            give(j, sums)
    else:
        sums = lax.fori_loop(0, parts, add, sums)
        lax.fori_loop(0, parts, give, sums)


def first_sum_kernel(annuli, in_ref, mark_ref, out_ref, give_ref):
    for j in range(in_ref.shape[0]):
        label = mark_ref[j : j + 1, :]
        said = in_ref[j, :1, :].astype(jnp.int32)
        give_ref[j : j + 1, :] = jnp.where(label < 0, said, label)
    add_and_give(annuli, in_ref, mark_ref, give_ref, out_ref)


def sum_kernel(annuli, in_ref, give_ref, out_ref):
    add_and_give(annuli, in_ref, give_ref, give_ref, out_ref)


def shards(npix, nfrm, curves, annulus_of_block, ref_blocks, keep_mask, start_basis):
    pixels, width = curves.shape
    nblocks, block = keep_mask.shape
    annuli, comps, _ = start_basis.shape
    chunk, frames, parts = pixels // nfrm, width * nfrm, npix * nfrm
    rows = comps * frames // LANES // parts
    narrow = jnp.bfloat16 if rows % 16 == 0 else jnp.float32

    smem = pl.BlockSpec(memory_space=pltpu.SMEM)
    vmem = pl.BlockSpec(memory_space=pltpu.VMEM)
    hbm = pl.BlockSpec(memory_space=pltpu.HBM)
    shape = jax.ShapeDtypeStruct

    def call(kernel, out, ins, outs, name, scratch=(), mib=32):
        return pl.pallas_call(
            kernel,
            out_shape=out,
            in_specs=ins,
            out_specs=outs,
            scratch_shapes=list(scratch),
            compiler_params=pltpu.CompilerParams(vmem_limit_bytes=mib * 1024 * 1024),
            name=name,
        )

    def rotate(x, shift):
        return lax.ppermute(x, "frm", [(i, (i + shift) % nfrm) for i in range(nfrm)])

    starts = [rotate(start_basis, shift) for shift in range(1, nfrm)]
    messages = call(
        pack_kernel,
        [shape((chunk, width), jnp.bfloat16)] * (nfrm - 1),
        [hbm],
        [vmem] * (nfrm - 1),
        "pack",
        [pltpu.SemaphoreType.DMA((nfrm - 1,))],
    )(curves)
    got = [rotate(message, shift) for shift, message in enumerate(messages, 1)]
    own, raw, weight, say, marks = call(
        functools.partial(own_kernel, block, parts // (npix * nblocks)),
        (
            shape((chunk, width), jnp.bfloat16),
            shape((comps, chunk), jnp.float32),
            shape((1, chunk), jnp.float32),
            shape((1, LANES), jnp.float32),
            shape((parts, LANES), jnp.int32),
        ),
        [smem, smem, vmem, hbm, hbm],
        (vmem, vmem, vmem, vmem, vmem),
        "own_part",
        [
            pltpu.VMEM((comps, width), jnp.bfloat16),
            pltpu.SMEM((npix * nblocks,), jnp.int32),
            pltpu.SemaphoreType.DMA((2,)),
        ],
    )(annulus_of_block, ref_blocks, keep_mask.reshape(nfrm, chunk), curves, start_basis)
    held = [own, *got]
    sent = call(
        functools.partial(first_kernel, block, nfrm),
        shape((parts, rows, LANES), jnp.float32),
        [smem] + [vmem] * (4 + 2 * (nfrm - 1)),
        vmem,
        "first_span",
    )(annulus_of_block, raw, weight, say, own, *got, *starts)

    give = None
    for step in range(ITERS):
        kind = narrow if step else jnp.float32
        taken = lax.all_to_all(sent, BOTH, 0, 0, tiled=True)
        total = shape((parts, rows, LANES), kind)
        if step == 0:
            total, give = call(
                functools.partial(first_sum_kernel, annuli),
                (total, shape((parts, LANES), jnp.int32)),
                [vmem, vmem],
                (vmem, vmem),
                "first_sum",
            )(taken, marks)
        else:
            total = call(
                functools.partial(sum_kernel, annuli), total, [vmem, vmem], vmem, "sum"
            )(taken, give)
        span = lax.all_to_all(total, BOTH, 0, 0, tiled=True)
        last = step == ITERS - 1
        sent = call(
            functools.partial(step_kernel, last, nfrm),
            shape((comps, chunk), jnp.float32) if last else shape((parts, rows, LANES), narrow),
            [vmem] * (2 + nfrm),
            vmem,
            "fit" if last else "step",
            [pltpu.VMEM((comps, frames), kind)],
        )(span, weight, *held)

    if nfrm == 2 and chunk == block:
        return call(
            place_kernel,
            shape((nblocks, comps, chunk), jnp.float32),
            [vmem, vmem],
            hbm,
            "place",
            [pltpu.SemaphoreType.DMA((2,))],
        )(sent, rotate(sent, 1))
    every = lax.all_gather(sent, "frm")
    return every.swapaxes(0, 1).reshape(comps, nblocks, block).swapaxes(0, 1)


def solution(mesh):
    in_specs = (P("pix", "frm"), P("pix"), P(), P("pix", None), P(None, None, "frm"))
    out_specs = P("pix", None, None)
    body = functools.partial(shards, mesh.shape["pix"], mesh.shape["frm"])
    return jax.shard_map(body, mesh=mesh, in_specs=in_specs, out_specs=out_specs, check_vma=False)
```

time: 108 us -> 105 us (0.972)
  waiting for transfers between devices: 2.62 us -> 1.08 us
  local copies, waits for them, and re-layouts: 2.84 us -> 1.59 us
    ppermute x2 -> x3, waiting for transfers between devices: 2.62 us -> 1.08 us  [rotate(): lax.ppermute(x, 'frm', [(i, (i + shift) % nfrm) for i in range(nfrm)])]
    unnamed x10 -> x12, local copies, waits for them, and re-layouts: 2.84 us -> 1.59 us
    pallas_call x7 -> x9, Pallas kernels: 8.94 us -> 9.29 us  [the longest x4 6.03 us: shards(): call(functools.partial(step_kernel, last, nfrm), shape((comps, chunk), jn...]
  transfers between devices with their start and end apart: 2 -> 3, of which waited for: 2 -> 2; matrix products, arithmetic and copies ran while one was open for 0% -> 0% of each run, Pallas kernels for 0% -> 1%
where the time goes in v3:
time: 105 us
  blocking collectives  90.9 us (87%)
  Pallas kernels  9.97 us (9%)
  local copies, waits for them, and re-layouts  1.59 us (2%)
  starting transfers between devices  1.2 us (1%)
  waiting for transfers between devices  1.08 us (1%)
    all_to_all x4, blocking collectives, shards(): taken = lax.all_to_all(sent, BOTH, 0, 0, tiled=True)  48.1 us
    all_to_all x4, blocking collectives, shards(): span = lax.all_to_all(total, BOTH, 0, 0, tiled=True)  42.8 us
    pallas_call x4, Pallas kernels, shards(): call(functools.partial(step_kernel, last, nfrm), shape((comps, chunk), jn...  6.03 us
  transfers between devices with their start and end apart: 3, of which 2 were waited for; matrix products, arithmetic and copies ran while one was open for 0% of the time, Pallas kernels for 1%

profile of v3, /device:TPU:0, one launch (start us, length us, event | category | flops | bytes accessed | tf_op | source)
XLA Modules:
  0.0 104.8 jit_solution(6614797230977209863)
XLA Ops:
  0.0 0.0 copy-start
  0.0 1.2 %copy-done = bf16[512,1024]{1,0:T(8,128)(2,1)S(1)} copy-done((bf16[512,1024]{1,0:T(8,128)(2,1)S(1)}, bf16[512,1024]{1,0:T(8,128)(2,1)}, u32[]{:S(2)}) %copy-start) | copy-done | bytes 1048600
  1.2 0.0 copy-start.2
  1.2 0.0 copy-start.1
  1.2 0.0 copy-start.3
  1.2 0.0 copy-start.4
  1.2 0.0 copy-start.5
  1.2 0.1 pack.1
  1.3 0.5 collective-permute-start
  1.8 0.3 copy-done.2
  2.2 0.5 collective-permute-start.1
  2.6 0.0 copy-done.1
  2.6 0.0 copy-done.3
  2.6 0.0 copy-done.4
  2.6 0.0 copy-done.5
  2.6 1.1 %own_part.1 = (bf16[256,1024]{1,0:T(8,128)(2,1)S(1)}, f32[32,256]{1,0:T(8,128)S(1)}, f32[1,256]{1,0:T(1,128)S(1)}, f32[1,128]{1,0:T(1,128)S(1)}, s32[32,128]{1,0:T(8,128)S(1)}) custom-call(s32[2]{0:T(128)S(1)} %copy-done.5, s32[4,8]{1,0:T(4,128)S(1)} %copy-done.3, s32[2,256]{1,0:T(2,128)S(1)} %copy-done.4, bf16[512,1024]{1,0:T(8,128)(2,1)S(1)} %copy-done.1, ...), custom_call_target="tpu_custom_call" | custom-call | tf_op jit(solution)/shard_map/own_part/pallas_call | solution.py:258
  3.7 0.1 collective-permute-done.1.refs_1_
  3.8 0.0 collective-permute-done.refs_0_.refs_1_
  3.8 1.3 %first_span.1 = f32[32,16,128]{2,1,0:T(8,128)S(1)} custom-call(s32[2]{0:T(128)S(1)} %copy-done.5, f32[32,256]{1,0:T(8,128)S(1)} %get-tuple-element.12.raw_ref, f32[1,256]{1,0:T(1,128)S(1)} %get-tuple-element.13.weight_ref, f32[1,128]{1,0:T(1,128)S(1)} %get-tuple-element.14.say_ref, bf16[256,1024]{1,0:T(8,128)(2,1)S(1)} %get-tuple-element.15.own_ref.refs_0_, ...), custom_call_target="tpu_custom_call" | custom-call | tf_op jit(solution)/shard_map/first_span/pallas_call | solution.py:277
  5.1 17.6 %all_to_all.40.in_ref = f32[32,16,128]{2,1,0:T(8,128)S(1)} all-to-all(f32[32,16,128]{2,1,0:T(8,128)S(1)} %first_span.1), channel_id=1, replica_groups=mesh['pix'=16,'frm'=2] {'pix','frm'}, dimensions={0} | all-to-all | bytes 524288 | tf_op jit(solution)/shard_map/all_to_all | solution.py:288
  22.7 0.2 first_sum.1
  22.9 12.8 %all_to_all.41.span_ref = f32[32,16,128]{2,1,0:T(8,128)S(1)} all-to-all(f32[32,16,128]{2,1,0:T(8,128)S(1)} %get-tuple-element.17), channel_id=1, replica_groups=mesh['pix'=16,'frm'=2] {'pix','frm'}, dimensions={0} | all-to-all | bytes 524288 | tf_op jit(solution)/shard_map/all_to_all | solution.py:302
  35.7 1.7 %step.3 = bf16[32,16,128]{2,1,0:T(8,128)(2,1)S(1)} custom-call(f32[32,16,128]{2,1,0:T(8,128)S(1)} %all_to_all.41.span_ref, f32[1,256]{1,0:T(1,128)S(1)} %get-tuple-element.13.weight_ref, bf16[256,1024]{1,0:T(8,128)(2,1)S(1)} %get-tuple-element.15.own_ref.refs_0_, bf16[256,1024]{1,0:T(8,128)(2,1)S(1)} %collective-permute-done.refs_0_.refs_1_), custom_call_target="tpu_custom_call" | custom-call | tf_op jit(solution)/shard_map/step/pallas_call | solution.py:304
  37.5 10.4 %all_to_all.42.in_ref = bf16[32,16,128]{2,1,0:T(8,128)(2,1)S(1)} all-to-all(bf16[32,16,128]{2,1,0:T(8,128)(2,1)S(1)} %step.3), channel_id=1, replica_groups=mesh['pix'=16,'frm'=2] {'pix','frm'}, dimensions={0} | all-to-all | bytes 262144 | tf_op jit(solution)/shard_map/all_to_all | solution.py:288
  47.9 0.2 sum.3
  48.1 10.0 %all_to_all.43.span_ref = bf16[32,16,128]{2,1,0:T(8,128)(2,1)S(1)} all-to-all(bf16[32,16,128]{2,1,0:T(8,128)(2,1)S(1)} %sum.3), channel_id=1, replica_groups=mesh['pix'=16,'frm'=2] {'pix','frm'}, dimensions={0} | all-to-all | bytes 262144 | tf_op jit(solution)/shard_map/all_to_all | solution.py:302
  58.1 1.5 %step.4 = bf16[32,16,128]{2,1,0:T(8,128)(2,1)S(1)} custom-call(bf16[32,16,128]{2,1,0:T(8,128)(2,1)S(1)} %all_to_all.43.span_ref, f32[1,256]{1,0:T(1,128)S(1)} %get-tuple-element.13.weight_ref, bf16[256,1024]{1,0:T(8,128)(2,1)S(1)} %get-tuple-element.15.own_ref.refs_0_, bf16[256,1024]{1,0:T(8,128)(2,1)S(1)} %collective-permute-done.refs_0_.refs_1_), custom_call_target="tpu_custom_call" | custom-call | tf_op jit(solution)/shard_map/step/pallas_call | solution.py:304
  59.6 10.0 %all_to_all.44.in_ref = bf16[32,16,128]{2,1,0:T(8,128)(2,1)S(1)} all-to-all(bf16[32,16,128]{2,1,0:T(8,128)(2,1)S(1)} %step.4), channel_id=1, replica_groups=mesh['pix'=16,'frm'=2] {'pix','frm'}, dimensions={0} | all-to-all | bytes 262144 | tf_op jit(solution)/shard_map/all_to_all | solution.py:288
  69.7 0.2 sum.4
  69.9 10.0 %all_to_all.45.span_ref = bf16[32,16,128]{2,1,0:T(8,128)(2,1)S(1)} all-to-all(bf16[32,16,128]{2,1,0:T(8,128)(2,1)S(1)} %sum.4), channel_id=1, replica_groups=mesh['pix'=16,'frm'=2] {'pix','frm'}, dimensions={0} | all-to-all | bytes 262144 | tf_op jit(solution)/shard_map/all_to_all | solution.py:302
  79.9 1.5 %step.5 = bf16[32,16,128]{2,1,0:T(8,128)(2,1)S(1)} custom-call(bf16[32,16,128]{2,1,0:T(8,128)(2,1)S(1)} %all_to_all.45.span_ref, f32[1,256]{1,0:T(1,128)S(1)} %get-tuple-element.13.weight_ref, bf16[256,1024]{1,0:T(8,128)(2,1)S(1)} %get-tuple-element.15.own_ref.refs_0_, bf16[256,1024]{1,0:T(8,128)(2,1)S(1)} %collective-permute-done.refs_0_.refs_1_), custom_call_target="tpu_custom_call" | custom-call | tf_op jit(solution)/shard_map/step/pallas_call | solution.py:304
  81.4 10.0 %all_to_all.46.in_ref = bf16[32,16,128]{2,1,0:T(8,128)(2,1)S(1)} all-to-all(bf16[32,16,128]{2,1,0:T(8,128)(2,1)S(1)} %step.5), channel_id=1, replica_groups=mesh['pix'=16,'frm'=2] {'pix','frm'}, dimensions={0} | all-to-all | bytes 262144 | tf_op jit(solution)/shard_map/all_to_all | solution.py:288
  91.4 0.2 sum.5
  91.6 10.0 %all_to_all.47.span_ref = bf16[32,16,128]{2,1,0:T(8,128)(2,1)S(1)} all-to-all(bf16[32,16,128]{2,1,0:T(8,128)(2,1)S(1)} %sum.5), channel_id=1, replica_groups=mesh['pix'=16,'frm'=2] {'pix','frm'}, dimensions={0} | all-to-all | bytes 262144 | tf_op jit(solution)/shard_map/all_to_all | solution.py:302
  101.6 1.3 %fit.1.own_ref = f32[32,256]{1,0:T(8,128)S(1)} custom-call(bf16[32,16,128]{2,1,0:T(8,128)(2,1)S(1)} %all_to_all.47.span_ref, f32[1,256]{1,0:T(1,128)S(1)} %get-tuple-element.13.weight_ref, bf16[256,1024]{1,0:T(8,128)(2,1)S(1)} %get-tuple-element.15.own_ref.refs_0_, bf16[256,1024]{1,0:T(8,128)(2,1)S(1)} %collective-permute-done.refs_0_.refs_1_), custom_call_target="tpu_custom_call" | custom-call | tf_op jit(solution)/shard_map/fit/pallas_call | solution.py:304
  103.0 0.2 collective-permute-start.2
  103.2 1.0 collective-permute-done.2.other_ref
  104.2 0.6 place.1
Async XLA Ops:
  0.0 1.2 %copy-start = (bf16[512,1024]{1,0:T(8,128)(2,1)S(1)}, bf16[512,1024]{1,0:T(8,128)(2,1)}, u32[]{:S(2)}) copy-start(bf16[512,1024]{1,0:T(8,128)(2,1)} %own_ref.1) | copy-start | bytes 3145732
  1.2 0.9 copy-start.2
  1.2 1.4 %copy-start.1 = (bf16[512,1024]{1,0:T(8,128)(2,1)S(1)}, bf16[512,1024]{1,0:T(8,128)(2,1)}, u32[]{:S(2)}) copy-start(bf16[512,1024]{1,0:T(8,128)(2,1)} %own_ref.1) | copy-start | bytes 3145732
  1.2 1.4 %copy-start.3 = (s32[4,8]{1,0:T(4,128)S(1)}, s32[4,8]{1,0:T(4,128)}, u32[]{:S(2)}) copy-start(s32[4,8]{1,0:T(4,128)} %listed_ref.1) | copy-start | bytes 388
  1.2 1.4 %copy-start.4 = (s32[2,256]{1,0:T(2,128)S(1)}, s32[2,256]{1,0:T(2,128)}, u32[]{:S(2)}) copy-start(s32[2,256]{1,0:T(2,128)} %keep_ref.1) | copy-start | bytes 6148
  1.2 1.4 %copy-start.5 = (s32[2]{0:T(128)S(1)}, s32[2]{0:T(128)}, u32[]{:S(2)}) copy-start(s32[2]{0:T(128)} %ann_ref.3) | copy-start | bytes 28
  1.3 2.5 %collective-permute-start = (bf16[256,1024]{1,0:T(8,128)(2,1)S(1)}, bf16[256,1024]{1,0:T(8,128)(2,1)S(1)}, u32[]{:S(2)}, u32[]{:S(2)}) collective-permute-start(bf16[256,1024]{1,0:T(8,128)(2,1)S(1)} %pack.1), channel_id=1, source_target_pairs={{0,1},{1,0},{2,3},{3,2},{4,5},{5,4},{6,7},{7,6},{8,9},{9,8},{10,11... | collective-permute-start | bytes 1572872 | tf_op jit(solution)/shard_map/ppermute | solution.py:246
  2.2 1.6 %collective-permute-start.1 = (bf16[4,32,1024]{2,1,0:T(8,128)(2,1)S(1)}, bf16[4,32,1024]{2,1,0:T(8,128)(2,1)S(1)}, u32[]{:S(2)}, u32[]{:S(2)}) collective-permute-start(bf16[4,32,1024]{2,1,0:T(8,128)(2,1)S(1)} %copy-done.2), channel_id=1, source_target_pairs={{0,1},{1,0},{2,3},{3,2},{4,5},{5,4},{6,7},{7,6},{8,9},{9,8},{10,11... | collective-permute-start | bytes 786440 | tf_op jit(solution)/shard_map/ppermute | solution.py:246
  103.0 1.2 %collective-permute-start.2 = (f32[32,256]{1,0:T(8,128)S(1)}, f32[32,256]{1,0:T(8,128)S(1)}, u32[]{:S(2)}, u32[]{:S(2)}) collective-permute-start(f32[32,256]{1,0:T(8,128)S(1)} %fit.1.own_ref), channel_id=1, source_target_pairs={{0,1},{1,0},{2,3},{3,2},{4,5},{5,4},{6,7},{7,6},{8,9},{9,8},{10,11... | collective-permute-start | bytes 98312 | tf_op jit(solution)/shard_map/ppermute | solution.py:246

commit v4 on v3

--- a/solution.py
+++ b/solution.py
@@ -15,23 +15,37 @@
 ROWS_TO_ROWS = (((1,), (1,)), ((), ()))
 
 
-def inverse_factor(gram):
+def solve_rows(gram, raw):
     k = gram.shape[0]
     rows = lax.broadcasted_iota(jnp.int32, (k, LANES), 0)
-    cols = lax.broadcasted_iota(jnp.int32, (k, LANES), 1)
-    wide = jnp.concatenate([gram, jnp.zeros((k, LANES - k), jnp.float32)], axis=1)
-    wide = wide + jnp.where(cols == rows + k, 1.0, 0.0)
+    low = jnp.concatenate([gram, jnp.zeros((k, LANES - k), jnp.float32)], axis=1)
+    wide = raw.shape[1] // LANES if raw.shape[1] % LANES == 0 else 1
+    size = raw.shape[1] // wide
+    right = [raw[:, t * size : (t + 1) * size] for t in range(wide)]
+    done = [[] for _ in right]
+    pivots = jnp.zeros((k, LANES), jnp.float32)
     for base in range(0, k, PANEL):
-        low, below = wide[base:, :], rows[base:, :]
+        below = rows[base:, :]
         panel = [jnp.broadcast_to(low[:, base + j : base + j + 1], low.shape) for j in range(PANEL)]
+        pivot = panel[0][:1, :]
         for j in range(PANEL):
-            factor = jnp.where(below > base + j, panel[j] * (1.0 / panel[j][j : j + 1, :]), 0.0)
+            inverse = 1.0 / pivot
+            pivots = jnp.where(rows == base + j, pivot, pivots)
+            if j + 1 < PANEL:
+                beside = panel[j + 1][j : j + 1, :]
+                pivot = panel[j + 1][j + 1 : j + 2, :] - beside * beside * inverse
+            factor = jnp.where(below > base + j, panel[j] * inverse, 0.0)
             for i in range(j + 1, PANEL):
                 panel[i] = panel[i] - factor * panel[i][j : j + 1, :]
-            low = low - factor * low[j : j + 1, :]
-        wide = jnp.concatenate([wide[:base, :], low], axis=0) if base else low
-    pivots = jnp.sum(jnp.where(cols == rows, wide, 0.0), axis=1, keepdims=True)
-    return wide[:, k : 2 * k] * lax.rsqrt(pivots)
+            if base + PANEL < k:
+                low = low - factor * low[j : j + 1, :]
+            right = [x - factor[:, :size] * x[j : j + 1, :] for x in right]
+        low = low[PANEL:, :]
+        for held, x in zip(done, right):
+            held.append(x[:PANEL, :])
+        right = [x[PANEL:, :] for x in right]
+    scale = lax.rsqrt(pivots)[:, :size]
+    return jnp.concatenate([jnp.concatenate(held, axis=0) * scale for held in done], axis=1)
 
 
 def pieces(wide):
@@ -159,7 +173,7 @@
         gram = lax.dot_general(
             span, span, ROWS_TO_ROWS, precision=EXACT, preferred_element_type=jnp.float32
         )
-    proj = jnp.dot(inverse_factor(gram), raw, precision=EXACT, preferred_element_type=jnp.float32)
+    proj = solve_rows(gram, raw)
     if last:
         out_ref[...] = proj
     else:

time: 105 us -> 104 us (level)
  Pallas kernels: 9.97 us -> 8.82 us
    pallas_call x4, Pallas kernels: 6.03 us -> 4.87 us  [shards(): call(functools.partial(step_kernel, last, nfrm), shape((comps, chunk), jn...]
where the time goes in v4:
time: 104 us
  blocking collectives  90.9 us (87%)
  Pallas kernels  8.82 us (8%)
  local copies, waits for them, and re-layouts  1.59 us (2%)
  starting transfers between devices  1.26 us (1%)
  waiting for transfers between devices  1.07 us (1%)
    all_to_all x4, blocking collectives, shards(): taken = lax.all_to_all(sent, BOTH, 0, 0, tiled=True)  48.1 us
    all_to_all x4, blocking collectives, shards(): span = lax.all_to_all(total, BOTH, 0, 0, tiled=True)  42.8 us
    pallas_call x4, Pallas kernels, shards(): call(functools.partial(step_kernel, last, nfrm), shape((comps, chunk), jn...  4.87 us
  transfers between devices with their start and end apart: 3, of which 2 were waited for; matrix products, arithmetic and copies ran while one was open for 0% of the time, Pallas kernels for 1%

profile of v4, /device:TPU:0, one launch (start us, length us, event | category | flops | bytes accessed | tf_op | source)
XLA Modules:
  0.0 103.7 jit_solution(18309073433193386655)
XLA Ops:
  0.0 0.0 copy-start
  0.0 1.2 %copy-done = bf16[512,1024]{1,0:T(8,128)(2,1)S(1)} copy-done((bf16[512,1024]{1,0:T(8,128)(2,1)S(1)}, bf16[512,1024]{1,0:T(8,128)(2,1)}, u32[]{:S(2)}) %copy-start) | copy-done | bytes 1048600
  1.2 0.0 copy-start.2
  1.2 0.0 copy-start.1
  1.2 0.0 copy-start.3
  1.2 0.0 copy-start.4
  1.2 0.0 copy-start.5
  1.2 0.1 pack.1
  1.3 0.5 collective-permute-start
  1.8 0.3 copy-done.2
  2.2 0.5 collective-permute-start.1
  2.6 0.0 copy-done.1
  2.6 0.0 copy-done.3
  2.6 0.0 copy-done.4
  2.6 0.0 copy-done.5
  2.6 1.1 %own_part.1 = (bf16[256,1024]{1,0:T(8,128)(2,1)S(1)}, f32[32,256]{1,0:T(8,128)S(1)}, f32[1,256]{1,0:T(1,128)S(1)}, f32[1,128]{1,0:T(1,128)S(1)}, s32[32,128]{1,0:T(8,128)S(1)}) custom-call(s32[2]{0:T(128)S(1)} %copy-done.5, s32[4,8]{1,0:T(4,128)S(1)} %copy-done.3, s32[2,256]{1,0:T(2,128)S(1)} %copy-done.4, bf16[512,1024]{1,0:T(8,128)(2,1)S(1)} %copy-done.1, ...), custom_call_target="tpu_custom_call" | custom-call | tf_op jit(solution)/shard_map/own_part/pallas_call | solution.py:272
  3.7 0.1 collective-permute-done.1.refs_1_
  3.8 0.0 collective-permute-done.refs_0_.refs_1_
  3.8 1.3 %first_span.1 = f32[32,16,128]{2,1,0:T(8,128)S(1)} custom-call(s32[2]{0:T(128)S(1)} %copy-done.5, f32[32,256]{1,0:T(8,128)S(1)} %get-tuple-element.12.raw_ref, f32[1,256]{1,0:T(1,128)S(1)} %get-tuple-element.13.weight_ref, f32[1,128]{1,0:T(1,128)S(1)} %get-tuple-element.14.say_ref, bf16[256,1024]{1,0:T(8,128)(2,1)S(1)} %get-tuple-element.15.own_ref.refs_0_, ...), custom_call_target="tpu_custom_call" | custom-call | tf_op jit(solution)/shard_map/first_span/pallas_call | solution.py:291
  5.1 17.6 %all_to_all.40.in_ref = f32[32,16,128]{2,1,0:T(8,128)S(1)} all-to-all(f32[32,16,128]{2,1,0:T(8,128)S(1)} %first_span.1), channel_id=1, replica_groups=mesh['pix'=16,'frm'=2] {'pix','frm'}, dimensions={0} | all-to-all | bytes 524288 | tf_op jit(solution)/shard_map/all_to_all | solution.py:302
  22.7 0.2 first_sum.1
  22.9 12.8 %all_to_all.41.span_ref = f32[32,16,128]{2,1,0:T(8,128)S(1)} all-to-all(f32[32,16,128]{2,1,0:T(8,128)S(1)} %get-tuple-element.17), channel_id=1, replica_groups=mesh['pix'=16,'frm'=2] {'pix','frm'}, dimensions={0} | all-to-all | bytes 524288 | tf_op jit(solution)/shard_map/all_to_all | solution.py:316
  35.7 1.4 %step.3 = bf16[32,16,128]{2,1,0:T(8,128)(2,1)S(1)} custom-call(f32[32,16,128]{2,1,0:T(8,128)S(1)} %all_to_all.41.span_ref, f32[1,256]{1,0:T(1,128)S(1)} %get-tuple-element.13.weight_ref, bf16[256,1024]{1,0:T(8,128)(2,1)S(1)} %get-tuple-element.15.own_ref.refs_0_, bf16[256,1024]{1,0:T(8,128)(2,1)S(1)} %collective-permute-done.refs_0_.refs_1_), custom_call_target="tpu_custom_call" | custom-call | tf_op jit(solution)/shard_map/step/pallas_call | solution.py:318
  37.2 10.5 %all_to_all.42.in_ref = bf16[32,16,128]{2,1,0:T(8,128)(2,1)S(1)} all-to-all(bf16[32,16,128]{2,1,0:T(8,128)(2,1)S(1)} %step.3), channel_id=1, replica_groups=mesh['pix'=16,'frm'=2] {'pix','frm'}, dimensions={0} | all-to-all | bytes 262144 | tf_op jit(solution)/shard_map/all_to_all | solution.py:302
  47.6 0.2 sum.3
  47.8 10.0 %all_to_all.43.span_ref = bf16[32,16,128]{2,1,0:T(8,128)(2,1)S(1)} all-to-all(bf16[32,16,128]{2,1,0:T(8,128)(2,1)S(1)} %sum.3), channel_id=1, replica_groups=mesh['pix'=16,'frm'=2] {'pix','frm'}, dimensions={0} | all-to-all | bytes 262144 | tf_op jit(solution)/shard_map/all_to_all | solution.py:316
  57.8 1.2 %step.4 = bf16[32,16,128]{2,1,0:T(8,128)(2,1)S(1)} custom-call(bf16[32,16,128]{2,1,0:T(8,128)(2,1)S(1)} %all_to_all.43.span_ref, f32[1,256]{1,0:T(1,128)S(1)} %get-tuple-element.13.weight_ref, bf16[256,1024]{1,0:T(8,128)(2,1)S(1)} %get-tuple-element.15.own_ref.refs_0_, bf16[256,1024]{1,0:T(8,128)(2,1)S(1)} %collective-permute-done.refs_0_.refs_1_), custom_call_target="tpu_custom_call" | custom-call | tf_op jit(solution)/shard_map/step/pallas_call | solution.py:318
  59.1 10.0 %all_to_all.44.in_ref = bf16[32,16,128]{2,1,0:T(8,128)(2,1)S(1)} all-to-all(bf16[32,16,128]{2,1,0:T(8,128)(2,1)S(1)} %step.4), channel_id=1, replica_groups=mesh['pix'=16,'frm'=2] {'pix','frm'}, dimensions={0} | all-to-all | bytes 262144 | tf_op jit(solution)/shard_map/all_to_all | solution.py:302
  69.1 0.2 sum.4
  69.3 10.0 %all_to_all.45.span_ref = bf16[32,16,128]{2,1,0:T(8,128)(2,1)S(1)} all-to-all(bf16[32,16,128]{2,1,0:T(8,128)(2,1)S(1)} %sum.4), channel_id=1, replica_groups=mesh['pix'=16,'frm'=2] {'pix','frm'}, dimensions={0} | all-to-all | bytes 262144 | tf_op jit(solution)/shard_map/all_to_all | solution.py:316
  79.3 1.2 %step.5 = bf16[32,16,128]{2,1,0:T(8,128)(2,1)S(1)} custom-call(bf16[32,16,128]{2,1,0:T(8,128)(2,1)S(1)} %all_to_all.45.span_ref, f32[1,256]{1,0:T(1,128)S(1)} %get-tuple-element.13.weight_ref, bf16[256,1024]{1,0:T(8,128)(2,1)S(1)} %get-tuple-element.15.own_ref.refs_0_, bf16[256,1024]{1,0:T(8,128)(2,1)S(1)} %collective-permute-done.refs_0_.refs_1_), custom_call_target="tpu_custom_call" | custom-call | tf_op jit(solution)/shard_map/step/pallas_call | solution.py:318
  80.5 10.0 %all_to_all.46.in_ref = bf16[32,16,128]{2,1,0:T(8,128)(2,1)S(1)} all-to-all(bf16[32,16,128]{2,1,0:T(8,128)(2,1)S(1)} %step.5), channel_id=1, replica_groups=mesh['pix'=16,'frm'=2] {'pix','frm'}, dimensions={0} | all-to-all | bytes 262144 | tf_op jit(solution)/shard_map/all_to_all | solution.py:302
  90.5 0.2 sum.5
  90.8 10.0 %all_to_all.47.span_ref = bf16[32,16,128]{2,1,0:T(8,128)(2,1)S(1)} all-to-all(bf16[32,16,128]{2,1,0:T(8,128)(2,1)S(1)} %sum.5), channel_id=1, replica_groups=mesh['pix'=16,'frm'=2] {'pix','frm'}, dimensions={0} | all-to-all | bytes 262144 | tf_op jit(solution)/shard_map/all_to_all | solution.py:316
  100.8 1.0 fit.1.own_ref
  101.8 0.3 collective-permute-start.2
  102.1 1.0 collective-permute-done.2.other_ref
  103.1 0.6 place.1
Async XLA Ops:
  0.0 1.2 %copy-start = (bf16[512,1024]{1,0:T(8,128)(2,1)S(1)}, bf16[512,1024]{1,0:T(8,128)(2,1)}, u32[]{:S(2)}) copy-start(bf16[512,1024]{1,0:T(8,128)(2,1)} %own_ref.1) | copy-start | bytes 3145732
  1.2 0.9 copy-start.2
  1.2 1.4 %copy-start.1 = (bf16[512,1024]{1,0:T(8,128)(2,1)S(1)}, bf16[512,1024]{1,0:T(8,128)(2,1)}, u32[]{:S(2)}) copy-start(bf16[512,1024]{1,0:T(8,128)(2,1)} %own_ref.1) | copy-start | bytes 3145732
  1.2 1.4 %copy-start.3 = (s32[4,8]{1,0:T(4,128)S(1)}, s32[4,8]{1,0:T(4,128)}, u32[]{:S(2)}) copy-start(s32[4,8]{1,0:T(4,128)} %listed_ref.1) | copy-start | bytes 388
  1.2 1.4 %copy-start.4 = (s32[2,256]{1,0:T(2,128)S(1)}, s32[2,256]{1,0:T(2,128)}, u32[]{:S(2)}) copy-start(s32[2,256]{1,0:T(2,128)} %keep_ref.1) | copy-start | bytes 6148
  1.2 1.4 %copy-start.5 = (s32[2]{0:T(128)S(1)}, s32[2]{0:T(128)}, u32[]{:S(2)}) copy-start(s32[2]{0:T(128)} %ann_ref.3) | copy-start | bytes 28
  1.3 2.5 %collective-permute-start = (bf16[256,1024]{1,0:T(8,128)(2,1)S(1)}, bf16[256,1024]{1,0:T(8,128)(2,1)S(1)}, u32[]{:S(2)}, u32[]{:S(2)}) collective-permute-start(bf16[256,1024]{1,0:T(8,128)(2,1)S(1)} %pack.1), channel_id=1, source_target_pairs={{0,1},{1,0},{2,3},{3,2},{4,5},{5,4},{6,7},{7,6},{8,9},{9,8},{10,11... | collective-permute-start | bytes 1572872 | tf_op jit(solution)/shard_map/ppermute | solution.py:260
  2.2 1.6 %collective-permute-start.1 = (bf16[4,32,1024]{2,1,0:T(8,128)(2,1)S(1)}, bf16[4,32,1024]{2,1,0:T(8,128)(2,1)S(1)}, u32[]{:S(2)}, u32[]{:S(2)}) collective-permute-start(bf16[4,32,1024]{2,1,0:T(8,128)(2,1)S(1)} %copy-done.2), channel_id=1, source_target_pairs={{0,1},{1,0},{2,3},{3,2},{4,5},{5,4},{6,7},{7,6},{8,9},{9,8},{10,11... | collective-permute-start | bytes 786440 | tf_op jit(solution)/shard_map/ppermute | solution.py:260
  101.8 1.3 %collective-permute-start.2 = (f32[32,256]{1,0:T(8,128)S(1)}, f32[32,256]{1,0:T(8,128)S(1)}, u32[]{:S(2)}, u32[]{:S(2)}) collective-permute-start(f32[32,256]{1,0:T(8,128)S(1)} %fit.1.own_ref), channel_id=1, source_target_pairs={{0,1},{1,0},{2,3},{3,2},{4,5},{5,4},{6,7},{7,6},{8,9},{9,8},{10,11... | collective-permute-start | bytes 98312 | tf_op jit(solution)/shard_map/ppermute | solution.py:260

commit v5 on v4

--- a/solution.py
+++ b/solution.py
@@ -72,11 +72,17 @@
             out_ref[first + (down * across + along)] = tile.astype(out_ref.dtype)
 
 
+def mine(curves, chunk):
+    if curves.shape[0] == chunk:
+        return curves[...]
+    return curves[pl.ds(pl.multiple_of(lax.axis_index("frm") * chunk, chunk), chunk), :]
+
+
 def span_of(proj, weight, held, sources, out_ref):
     proj_bf = (proj * weight).astype(jnp.bfloat16)
     width = held[0].shape[1] // LANES
     for curves, source in zip(held, sources):
-        span = jnp.dot(proj_bf, curves[...], preferred_element_type=jnp.float32)
+        span = jnp.dot(proj_bf, mine(curves, proj.shape[1]), preferred_element_type=jnp.float32)
         yield span, source * width, width * len(held)
 
 
@@ -100,41 +106,43 @@
         copy.wait()
 
 
+def entry(row_ref, at):
+    lanes = lax.broadcasted_iota(jnp.int32, row_ref.shape, 1)
+    return jnp.sum(jnp.where(lanes == at, row_ref[...], 0).astype(jnp.float32)).astype(jnp.int32)
+
+
+def pick_kernel(block, chunk, ann_ref, start_ref, *out_refs):
+    others = len(out_refs) + 1
+    for shift, out_ref in enumerate(out_refs, 1):
+        target = lax.rem(lax.axis_index("frm") + shift, others)
+        out_ref[...] = start_ref[entry(ann_ref, target * chunk // block)]
+
+
 def own_kernel(
-    block, chunks, ann_ref, listed_ref, keep_ref, all_ref, start_ref,
-    own_ref, raw_ref, weight_ref, say_ref, mark_ref, basis, table, sems,
+    block, others, chunks, ann_ref, listed_ref, keep_ref, own_ref, start_ref,
+    raw_ref, weight_ref, say_ref, mark_ref,
 ):
     pix, frm = lax.axis_index("pix"), lax.axis_index("frm")
-    chunk = own_ref.shape[0]
-    rows = pl.ds(pl.multiple_of(frm * chunk, chunk), chunk)
-    place = frm * chunk // block
-    label = ann_ref[place]
-    curves = pltpu.make_async_copy(all_ref.at[rows], own_ref, sems.at[0])
-    start = pltpu.make_async_copy(start_ref.at[label], basis, sems.at[1])
-    curves.start()
-    start.start()
-    for b in range(table.shape[0]):
-        table[b] = -1
+    chunk = raw_ref.shape[1]
+    label = entry(ann_ref, frm * chunk // block)
+    raw_ref[...] = dot_rows(start_ref[label], mine(own_ref, chunk))
+    blocks = lax.broadcasted_iota(jnp.int32, mark_ref.shape, 0) // chunks
+    marks = jnp.full(mark_ref.shape, -1, jnp.int32)
     for a in range(listed_ref.shape[0]):
-        for entry in range(listed_ref.shape[1]):
-            table[listed_ref[a, entry]] = a
-    for j in range(mark_ref.shape[0]):
-        mark_ref[j : j + 1, :] = jnp.full((1, LANES), table[j // chunks], jnp.int32)
-    listed = (table[pix * ann_ref.shape[0] + place] >= 0).astype(jnp.int32)
+        for at in range(listed_ref.shape[1]):
+            marks = jnp.where(blocks == listed_ref[a : a + 1, at : at + 1], a, marks)
+    mark_ref[...] = marks
+    listed = mark_ref[pl.ds(pix * others + frm, 1), :] >= 0
     kept = keep_ref[pl.ds(frm, 1), :]
-    weight_ref[...] = jnp.where(kept == 1, listed, 0).astype(jnp.float32)
-    say_ref[...] = jnp.full((1, LANES), (1 - listed) * label, jnp.int32).astype(jnp.float32)
-    curves.wait()
-    start.wait()
-    raw_ref[...] = dot_rows(basis[...], own_ref[...])
-
-
-def first_kernel(block, others, ann_ref, raw_ref, weight_ref, say_ref, own_ref, *refs):
+    weight_ref[...] = jnp.where((kept == 1) & listed[:, :1], 1.0, 0.0)
+    say_ref[...] = jnp.where(listed, 0, label).astype(jnp.float32)
+
+
+def first_kernel(others, raw_ref, weight_ref, say_ref, own_ref, *refs):
     got, starts, out_ref = refs[: others - 1], refs[others - 1 : -1], refs[-1]
-    label = ann_ref[lax.axis_index("frm") * own_ref.shape[0] // block]
     proj = raw_ref[...]
     for curves, start in zip(got, starts):
-        proj = proj + dot_rows(start[label], curves[...])
+        proj = proj + dot_rows(start[...], curves[...])
     held, weight = (own_ref, *got), weight_ref[...]
     for span, first, across in span_of(proj, weight, held, frame_order(others), out_ref):
         store_tiles(
@@ -160,13 +168,14 @@
         down, along = j // across * rows, j % across * LANES
         whole[down : down + rows, along : along + LANES] = span_ref[j]
     span, sources = whole[...], frame_order(others)
-    raw = jnp.zeros((comps, held[0].shape[0]), jnp.float32)
+    chunk = weight_ref.shape[1]
+    raw = jnp.zeros((comps, chunk), jnp.float32)
     for curves, source in zip(held, sources):
         part = whole[:, pl.ds(pl.multiple_of(source * width, LANES), width)]
         if span.dtype == jnp.bfloat16:
-            raw = raw + dot_rows(part, curves[...])
+            raw = raw + dot_rows(part, mine(curves, chunk))
         else:
-            raw = raw + fold(dot_rows(pieces(part), curves[...]), comps)
+            raw = raw + fold(dot_rows(pieces(part), mine(curves, chunk)), comps)
     if span.dtype == jnp.bfloat16:
         gram = dot_rows(span, span)
     else:
@@ -240,7 +249,7 @@
     rows = comps * frames // LANES // parts
     narrow = jnp.bfloat16 if rows % 16 == 0 else jnp.float32
 
-    smem = pl.BlockSpec(memory_space=pltpu.SMEM)
+    labels = annulus_of_block.reshape(1, nblocks)
     vmem = pl.BlockSpec(memory_space=pltpu.VMEM)
     hbm = pl.BlockSpec(memory_space=pltpu.HBM)
     shape = jax.ShapeDtypeStruct
@@ -259,7 +268,6 @@
     def rotate(x, shift):
         return lax.ppermute(x, "frm", [(i, (i + shift) % nfrm) for i in range(nfrm)])
 
-    starts = [rotate(start_basis, shift) for shift in range(1, nfrm)]
     messages = call(
         pack_kernel,
         [shape((chunk, width), jnp.bfloat16)] * (nfrm - 1),
@@ -269,32 +277,34 @@
         [pltpu.SemaphoreType.DMA((nfrm - 1,))],
     )(curves)
     got = [rotate(message, shift) for shift, message in enumerate(messages, 1)]
-    own, raw, weight, say, marks = call(
-        functools.partial(own_kernel, block, parts // (npix * nblocks)),
+    picks = call(
+        functools.partial(pick_kernel, block, chunk),
+        [shape((comps, width), jnp.bfloat16)] * (nfrm - 1),
+        [vmem, vmem],
+        [vmem] * (nfrm - 1),
+        "pick",
+    )(labels, start_basis)
+    starts = [rotate(pick, shift) for shift, pick in enumerate(picks, 1)]
+    raw, weight, say, marks = call(
+        functools.partial(own_kernel, block, nfrm, parts // (npix * nblocks)),
         (
-            shape((chunk, width), jnp.bfloat16),
             shape((comps, chunk), jnp.float32),
             shape((1, chunk), jnp.float32),
             shape((1, LANES), jnp.float32),
             shape((parts, LANES), jnp.int32),
         ),
-        [smem, smem, vmem, hbm, hbm],
-        (vmem, vmem, vmem, vmem, vmem),
+        [vmem] * 5,
+        (vmem, vmem, vmem, vmem),
         "own_part",
-        [
-            pltpu.VMEM((comps, width), jnp.bfloat16),
-            pltpu.SMEM((npix * nblocks,), jnp.int32),
-            pltpu.SemaphoreType.DMA((2,)),
-        ],
-    )(annulus_of_block, ref_blocks, keep_mask.reshape(nfrm, chunk), curves, start_basis)
-    held = [own, *got]
+    )(labels, ref_blocks, keep_mask.reshape(nfrm, chunk), curves, start_basis)
+    held = [curves, *got]
     sent = call(
-        functools.partial(first_kernel, block, nfrm),
+        functools.partial(first_kernel, nfrm),
         shape((parts, rows, LANES), jnp.float32),
-        [smem] + [vmem] * (4 + 2 * (nfrm - 1)),
+        [vmem] * (4 + 2 * (nfrm - 1)),
         vmem,
         "first_span",
-    )(annulus_of_block, raw, weight, say, own, *got, *starts)
+    )(raw, weight, say, curves, *got, *starts)
 
     give = None
     for step in range(ITERS):

time: 104 us -> 103 us (level)
  Pallas kernels: 8.82 us -> 7.65 us
    pallas_call x2 -> x3, Pallas kernels: 2.33 us -> 1.19 us  [the longest x1 0.73 us: shards(): call(functools.partial(first_kernel, nfrm), shape((parts, rows, LANES), j...]
  transfers between devices with their start and end apart: 3 -> 3, of which waited for: 2 -> 2; matrix products, arithmetic and copies ran while one was open for 0% -> 0% of each run, Pallas kernels for 1% -> 0%
where the time goes in v5:
time: 103 us
  blocking collectives  90.9 us (88%)
  Pallas kernels  7.65 us (7%)
  local copies, waits for them, and re-layouts  1.71 us (2%)
  waiting for transfers between devices  1.48 us (1%)
  starting transfers between devices  1.3 us (1%)
    all_to_all x4, blocking collectives, shards(): taken = lax.all_to_all(sent, BOTH, 0, 0, tiled=True)  48.1 us
    all_to_all x4, blocking collectives, shards(): span = lax.all_to_all(total, BOTH, 0, 0, tiled=True)  42.8 us
    pallas_call x4, Pallas kernels, shards(): call(functools.partial(step_kernel, last, nfrm), shape((comps, chunk), jn...  4.87 us
  transfers between devices with their start and end apart: 3, of which 2 were waited for; matrix products, arithmetic and copies ran while one was open for 0% of the time, Pallas kernels for 0%

profile of v5, /device:TPU:0, one launch (start us, length us, event | category | flops | bytes accessed | tf_op | source)
XLA Modules:
  0.0 103.1 jit_solution(9593919198728734362)
XLA Ops:
  0.0 0.0 copy-start
  0.0 1.2 %copy-done = bf16[512,1024]{1,0:T(8,128)(2,1)S(1)} copy-done((bf16[512,1024]{1,0:T(8,128)(2,1)S(1)}, bf16[512,1024]{1,0:T(8,128)(2,1)}, u32[]{:S(2)}) %copy-start) | copy-done | bytes 1048600
  1.2 0.0 copy-start.2
  1.2 0.0 copy-start.1
  1.3 0.0 copy-start.5
  1.3 0.5 collective-permute-start
  1.8 0.4 copy-done.2
  2.2 0.0 copy-done.5
  2.2 0.0 copy-start.3
  2.2 0.0 copy-start.4
  2.2 0.1 pick.1
  2.3 0.5 collective-permute-start.1
  2.8 0.0 copy-done.1
  2.8 0.1 copy-done.3
  2.9 0.0 copy-done.4
  3.0 0.3 own_part.1
  3.3 0.5 collective-permute-done.1.refs_1_
  3.7 0.0 collective-permute-done.refs_0_.refs_1_
  3.8 0.7 first_span.1
  4.5 17.6 %all_to_all.40.in_ref = f32[32,16,128]{2,1,0:T(8,128)S(1)} all-to-all(f32[32,16,128]{2,1,0:T(8,128)S(1)} %first_span.1), channel_id=1, replica_groups=mesh['pix'=16,'frm'=2] {'pix','frm'}, dimensions={0} | all-to-all | bytes 524288 | tf_op jit(solution)/shard_map/all_to_all | solution.py:312
  22.1 0.2 first_sum.1
  22.3 12.8 %all_to_all.41.span_ref = f32[32,16,128]{2,1,0:T(8,128)S(1)} all-to-all(f32[32,16,128]{2,1,0:T(8,128)S(1)} %get-tuple-element.15), channel_id=1, replica_groups=mesh['pix'=16,'frm'=2] {'pix','frm'}, dimensions={0} | all-to-all | bytes 524288 | tf_op jit(solution)/shard_map/all_to_all | solution.py:326
  35.1 1.4 %step.3 = bf16[32,16,128]{2,1,0:T(8,128)(2,1)S(1)} custom-call(f32[32,16,128]{2,1,0:T(8,128)S(1)} %all_to_all.41.span_ref, f32[1,256]{1,0:T(1,128)S(1)} %get-tuple-element.12.weight_ref, bf16[512,1024]{1,0:T(8,128)(2,1)S(1)} %copy-done.1, bf16[256,1024]{1,0:T(8,128)(2,1)S(1)} %collective-permute-done.refs_0_.refs_1_), custom_call_target="tpu_custom_call" | custom-call | tf_op jit(solution)/shard_map/step/pallas_call | solution.py:328
  36.6 10.5 %all_to_all.42.in_ref = bf16[32,16,128]{2,1,0:T(8,128)(2,1)S(1)} all-to-all(bf16[32,16,128]{2,1,0:T(8,128)(2,1)S(1)} %step.3), channel_id=1, replica_groups=mesh['pix'=16,'frm'=2] {'pix','frm'}, dimensions={0} | all-to-all | bytes 262144 | tf_op jit(solution)/shard_map/all_to_all | solution.py:312
  47.0 0.2 sum.3
  47.2 10.0 %all_to_all.43.span_ref = bf16[32,16,128]{2,1,0:T(8,128)(2,1)S(1)} all-to-all(bf16[32,16,128]{2,1,0:T(8,128)(2,1)S(1)} %sum.3), channel_id=1, replica_groups=mesh['pix'=16,'frm'=2] {'pix','frm'}, dimensions={0} | all-to-all | bytes 262144 | tf_op jit(solution)/shard_map/all_to_all | solution.py:326
  57.2 1.2 %step.4 = bf16[32,16,128]{2,1,0:T(8,128)(2,1)S(1)} custom-call(bf16[32,16,128]{2,1,0:T(8,128)(2,1)S(1)} %all_to_all.43.span_ref, f32[1,256]{1,0:T(1,128)S(1)} %get-tuple-element.12.weight_ref, bf16[512,1024]{1,0:T(8,128)(2,1)S(1)} %copy-done.1, bf16[256,1024]{1,0:T(8,128)(2,1)S(1)} %collective-permute-done.refs_0_.refs_1_), custom_call_target="tpu_custom_call" | custom-call | tf_op jit(solution)/shard_map/step/pallas_call | solution.py:328
  58.4 10.0 %all_to_all.44.in_ref = bf16[32,16,128]{2,1,0:T(8,128)(2,1)S(1)} all-to-all(bf16[32,16,128]{2,1,0:T(8,128)(2,1)S(1)} %step.4), channel_id=1, replica_groups=mesh['pix'=16,'frm'=2] {'pix','frm'}, dimensions={0} | all-to-all | bytes 262144 | tf_op jit(solution)/shard_map/all_to_all | solution.py:312
  68.5 0.2 sum.4
  68.7 10.0 %all_to_all.45.span_ref = bf16[32,16,128]{2,1,0:T(8,128)(2,1)S(1)} all-to-all(bf16[32,16,128]{2,1,0:T(8,128)(2,1)S(1)} %sum.4), channel_id=1, replica_groups=mesh['pix'=16,'frm'=2] {'pix','frm'}, dimensions={0} | all-to-all | bytes 262144 | tf_op jit(solution)/shard_map/all_to_all | solution.py:326
  78.7 1.2 %step.5 = bf16[32,16,128]{2,1,0:T(8,128)(2,1)S(1)} custom-call(bf16[32,16,128]{2,1,0:T(8,128)(2,1)S(1)} %all_to_all.45.span_ref, f32[1,256]{1,0:T(1,128)S(1)} %get-tuple-element.12.weight_ref, bf16[512,1024]{1,0:T(8,128)(2,1)S(1)} %copy-done.1, bf16[256,1024]{1,0:T(8,128)(2,1)S(1)} %collective-permute-done.refs_0_.refs_1_), custom_call_target="tpu_custom_call" | custom-call | tf_op jit(solution)/shard_map/step/pallas_call | solution.py:328
  79.9 10.0 %all_to_all.46.in_ref = bf16[32,16,128]{2,1,0:T(8,128)(2,1)S(1)} all-to-all(bf16[32,16,128]{2,1,0:T(8,128)(2,1)S(1)} %step.5), channel_id=1, replica_groups=mesh['pix'=16,'frm'=2] {'pix','frm'}, dimensions={0} | all-to-all | bytes 262144 | tf_op jit(solution)/shard_map/all_to_all | solution.py:312
  89.9 0.2 sum.5
  90.2 10.0 %all_to_all.47.span_ref = bf16[32,16,128]{2,1,0:T(8,128)(2,1)S(1)} all-to-all(bf16[32,16,128]{2,1,0:T(8,128)(2,1)S(1)} %sum.5), channel_id=1, replica_groups=mesh['pix'=16,'frm'=2] {'pix','frm'}, dimensions={0} | all-to-all | bytes 262144 | tf_op jit(solution)/shard_map/all_to_all | solution.py:326
  100.2 1.0 %fit.1.own_ref = f32[32,256]{1,0:T(8,128)S(1)} custom-call(bf16[32,16,128]{2,1,0:T(8,128)(2,1)S(1)} %all_to_all.47.span_ref, f32[1,256]{1,0:T(1,128)S(1)} %get-tuple-element.12.weight_ref, bf16[512,1024]{1,0:T(8,128)(2,1)S(1)} %copy-done.1, bf16[256,1024]{1,0:T(8,128)(2,1)S(1)} %collective-permute-done.refs_0_.refs_1_), custom_call_target="tpu_custom_call" | custom-call | tf_op jit(solution)/shard_map/fit/pallas_call | solution.py:328
  101.2 0.3 collective-permute-start.2
  101.5 1.0 collective-permute-done.2.other_ref
  102.5 0.6 place.1
  (1 shorter events, 0.0 us)
Async XLA Ops:
  0.0 1.2 %copy-start = (bf16[512,1024]{1,0:T(8,128)(2,1)S(1)}, bf16[512,1024]{1,0:T(8,128)(2,1)}, u32[]{:S(2)}) copy-start(bf16[512,1024]{1,0:T(8,128)(2,1)} %refs_0_.7) | copy-start | bytes 3145732
  1.2 0.9 copy-start.2
  1.2 1.6 %copy-start.1 = (bf16[512,1024]{1,0:T(8,128)(2,1)S(1)}, bf16[512,1024]{1,0:T(8,128)(2,1)}, u32[]{:S(2)}) copy-start(bf16[512,1024]{1,0:T(8,128)(2,1)} %refs_0_.7) | copy-start | bytes 3145732
  1.3 0.9 copy-start.5
  1.3 2.5 %collective-permute-start = (bf16[256,1024]{1,0:T(8,128)(2,1)S(1)}, bf16[256,1024]{1,0:T(8,128)(2,1)S(1)}, u32[]{:S(2)}, u32[]{:S(2)}) collective-permute-start(bf16[256,1024]{1,0:T(8,128)(2,1)S(1)} %pack.1), channel_id=1, source_target_pairs={{0,1},{1,0},{2,3},{3,2},{4,5},{5,4},{6,7},{7,6},{8,9},{9,8},{10,11... | collective-permute-start | bytes 1572872 | tf_op jit(solution)/shard_map/ppermute | solution.py:269
  2.2 0.8 copy-start.3
  2.2 0.8 copy-start.4
  2.3 1.4 %collective-permute-start.1 = (bf16[32,1024]{1,0:T(8,128)(2,1)S(1)}, bf16[32,1024]{1,0:T(8,128)(2,1)S(1)}, u32[]{:S(2)}, u32[]{:S(2)}) collective-permute-start(bf16[32,1024]{1,0:T(8,128)(2,1)S(1)} %pick.1), channel_id=1, source_target_pairs={{0,1},{1,0},{2,3},{3,2},{4,5},{5,4},{6,7},{7,6},{8,9},{9,8},{10,11... | collective-permute-start | bytes 196616 | tf_op jit(solution)/shard_map/ppermute | solution.py:269
  101.2 1.3 %collective-permute-start.2 = (f32[32,256]{1,0:T(8,128)S(1)}, f32[32,256]{1,0:T(8,128)S(1)}, u32[]{:S(2)}, u32[]{:S(2)}) collective-permute-start(f32[32,256]{1,0:T(8,128)S(1)} %fit.1.own_ref), channel_id=1, source_target_pairs={{0,1},{1,0},{2,3},{3,2},{4,5},{5,4},{6,7},{7,6},{8,9},{9,8},{10,11... | collective-permute-start | bytes 98312 | tf_op jit(solution)/shard_map/ppermute | solution.py:269

commit v6 on v5

--- a/solution.py
+++ b/solution.py
@@ -10,7 +10,7 @@
 ITERS = 4
 LANES = 128
 PANEL = 16
-BOTH = ("pix", "frm")
+BOTH = ("frm", "pix")
 EXACT = lax.Precision.HIGHEST
 ROWS_TO_ROWS = (((1,), (1,)), ((), ()))
 
@@ -119,20 +119,22 @@
 
 
 def own_kernel(
-    block, others, chunks, ann_ref, listed_ref, keep_ref, own_ref, start_ref,
+    block, others, ann_ref, listed_ref, keep_ref, own_ref, start_ref,
     raw_ref, weight_ref, say_ref, mark_ref,
 ):
     pix, frm = lax.axis_index("pix"), lax.axis_index("frm")
     chunk = raw_ref.shape[1]
     label = entry(ann_ref, frm * chunk // block)
     raw_ref[...] = dot_rows(start_ref[label], mine(own_ref, chunk))
-    blocks = lax.broadcasted_iota(jnp.int32, mark_ref.shape, 0) // chunks
+    npix = mark_ref.shape[0] // others
+    place = lax.broadcasted_iota(jnp.int32, mark_ref.shape, 0)
+    blocks = place % npix * ann_ref.shape[1] + place // npix * chunk // block
     marks = jnp.full(mark_ref.shape, -1, jnp.int32)
     for a in range(listed_ref.shape[0]):
         for at in range(listed_ref.shape[1]):
             marks = jnp.where(blocks == listed_ref[a : a + 1, at : at + 1], a, marks)
     mark_ref[...] = marks
-    listed = mark_ref[pl.ds(pix * others + frm, 1), :] >= 0
+    listed = mark_ref[pl.ds(frm * npix + pix, 1), :] >= 0
     kept = keep_ref[pl.ds(frm, 1), :]
     weight_ref[...] = jnp.where((kept == 1) & listed[:, :1], 1.0, 0.0)
     say_ref[...] = jnp.where(listed, 0, label).astype(jnp.float32)
@@ -168,6 +170,12 @@
         down, along = j // across * rows, j % across * LANES
         whole[down : down + rows, along : along + LANES] = span_ref[j]
     span, sources = whole[...], frame_order(others)
+    if span.dtype == jnp.bfloat16:
+        gram = dot_rows(span, span)
+    else:
+        gram = lax.dot_general(
+            span, span, ROWS_TO_ROWS, precision=EXACT, preferred_element_type=jnp.float32
+        )
     chunk = weight_ref.shape[1]
     raw = jnp.zeros((comps, chunk), jnp.float32)
     for curves, source in zip(held, sources):
@@ -176,12 +184,6 @@
             raw = raw + dot_rows(part, mine(curves, chunk))
         else:
             raw = raw + fold(dot_rows(pieces(part), mine(curves, chunk)), comps)
-    if span.dtype == jnp.bfloat16:
-        gram = dot_rows(span, span)
-    else:
-        gram = lax.dot_general(
-            span, span, ROWS_TO_ROWS, precision=EXACT, preferred_element_type=jnp.float32
-        )
     proj = solve_rows(gram, raw)
     if last:
         out_ref[...] = proj
@@ -286,7 +288,7 @@
     )(labels, start_basis)
     starts = [rotate(pick, shift) for shift, pick in enumerate(picks, 1)]
     raw, weight, say, marks = call(
-        functools.partial(own_kernel, block, nfrm, parts // (npix * nblocks)),
+        functools.partial(own_kernel, block, nfrm),
         (
             shape((comps, chunk), jnp.float32),
             shape((1, chunk), jnp.float32),

time: 103 us -> 103 us (level)
  no operation moved by 1% of the time
where the time goes in v6:
time: 103 us; the launch traced here: 102 us
  blocking collectives  90.3 us (88%)
  Pallas kernels  7.37 us (7%)
  local copies, waits for them, and re-layouts  1.71 us (2%)
  waiting for transfers between devices  1.66 us (2%)
  starting transfers between devices  1.11 us (1%)
    all_to_all x4, blocking collectives, shards(): taken = lax.all_to_all(sent, BOTH, 0, 0, tiled=True)  47.7 us
    all_to_all x4, blocking collectives, shards(): span = lax.all_to_all(total, BOTH, 0, 0, tiled=True)  42.6 us
    pallas_call x4, Pallas kernels, shards(): call(functools.partial(step_kernel, last, nfrm), shape((comps, chunk), jn...  4.57 us
  transfers between devices with their start and end apart: 3, of which 2 were waited for; matrix products, arithmetic and copies ran while one was open for 0% of the time, Pallas kernels for 0%

profile of v6, /device:TPU:0, one launch (start us, length us, event | category | flops | bytes accessed | tf_op | source)
XLA Modules:
  0.0 102.2 jit_solution(13242335819429032126)
XLA Ops:
  0.0 0.0 copy-start
  0.0 1.2 %copy-done = bf16[512,1024]{1,0:T(8,128)(2,1)S(1)} copy-done((bf16[512,1024]{1,0:T(8,128)(2,1)S(1)}, bf16[512,1024]{1,0:T(8,128)(2,1)}, u32[]{:S(2)}) %copy-start) | copy-done | bytes 1048600
  1.2 0.0 copy-start.2
  1.2 0.0 copy-start.1
  1.3 0.0 copy-start.5
  1.3 0.5 collective-permute-start
  1.8 0.4 copy-done.2
  2.2 0.0 copy-done.5
  2.2 0.0 copy-start.3
  2.2 0.0 copy-start.4
  2.2 0.1 pick.1
  2.3 0.5 collective-permute-start.1
  2.8 0.0 copy-done.1
  2.8 0.1 copy-done.3
  2.9 0.0 copy-done.4
  3.0 0.3 own_part.1
  3.3 0.5 collective-permute-done.1.refs_1_
  3.7 0.0 collective-permute-done.refs_0_.refs_1_
  3.8 0.7 first_span.1
  4.5 18.2 %all_to_all.40.in_ref = f32[32,16,128]{2,1,0:T(8,128)S(1)} all-to-all(f32[32,16,128]{2,1,0:T(8,128)S(1)} %first_span.1), channel_id=1, replica_groups=mesh['pix'=16,'frm'=2] {'frm','pix'}, dimensions={0} | all-to-all | bytes 524288 | tf_op jit(solution)/shard_map/all_to_all | solution.py:314
  22.7 0.2 first_sum.1
  22.9 12.9 %all_to_all.41.span_ref = f32[32,16,128]{2,1,0:T(8,128)S(1)} all-to-all(f32[32,16,128]{2,1,0:T(8,128)S(1)} %get-tuple-element.15), channel_id=1, replica_groups=mesh['pix'=16,'frm'=2] {'frm','pix'}, dimensions={0} | all-to-all | bytes 524288 | tf_op jit(solution)/shard_map/all_to_all | solution.py:328
  35.9 1.4 %step.3 = bf16[32,16,128]{2,1,0:T(8,128)(2,1)S(1)} custom-call(f32[32,16,128]{2,1,0:T(8,128)S(1)} %all_to_all.41.span_ref, f32[1,256]{1,0:T(1,128)S(1)} %get-tuple-element.12.weight_ref, bf16[512,1024]{1,0:T(8,128)(2,1)S(1)} %copy-done.1, bf16[256,1024]{1,0:T(8,128)(2,1)S(1)} %collective-permute-done.refs_0_.refs_1_), custom_call_target="tpu_custom_call" | custom-call | tf_op jit(solution)/shard_map/step/pallas_call | solution.py:330
  37.3 9.6 %all_to_all.42.in_ref = bf16[32,16,128]{2,1,0:T(8,128)(2,1)S(1)} all-to-all(bf16[32,16,128]{2,1,0:T(8,128)(2,1)S(1)} %step.3), channel_id=1, replica_groups=mesh['pix'=16,'frm'=2] {'frm','pix'}, dimensions={0} | all-to-all | bytes 262144 | tf_op jit(solution)/shard_map/all_to_all | solution.py:314
  46.9 0.2 sum.3
  47.1 9.8 %all_to_all.43.span_ref = bf16[32,16,128]{2,1,0:T(8,128)(2,1)S(1)} all-to-all(bf16[32,16,128]{2,1,0:T(8,128)(2,1)S(1)} %sum.3), channel_id=1, replica_groups=mesh['pix'=16,'frm'=2] {'frm','pix'}, dimensions={0} | all-to-all | bytes 262144 | tf_op jit(solution)/shard_map/all_to_all | solution.py:328
  56.9 1.2 %step.4 = bf16[32,16,128]{2,1,0:T(8,128)(2,1)S(1)} custom-call(bf16[32,16,128]{2,1,0:T(8,128)(2,1)S(1)} %all_to_all.43.span_ref, f32[1,256]{1,0:T(1,128)S(1)} %get-tuple-element.12.weight_ref, bf16[512,1024]{1,0:T(8,128)(2,1)S(1)} %copy-done.1, bf16[256,1024]{1,0:T(8,128)(2,1)S(1)} %collective-permute-done.refs_0_.refs_1_), custom_call_target="tpu_custom_call" | custom-call | tf_op jit(solution)/shard_map/step/pallas_call | solution.py:330
  58.1 9.9 %all_to_all.44.in_ref = bf16[32,16,128]{2,1,0:T(8,128)(2,1)S(1)} all-to-all(bf16[32,16,128]{2,1,0:T(8,128)(2,1)S(1)} %step.4), channel_id=1, replica_groups=mesh['pix'=16,'frm'=2] {'frm','pix'}, dimensions={0} | all-to-all | bytes 262144 | tf_op jit(solution)/shard_map/all_to_all | solution.py:314
  68.0 0.2 sum.4
  68.3 9.9 %all_to_all.45.span_ref = bf16[32,16,128]{2,1,0:T(8,128)(2,1)S(1)} all-to-all(bf16[32,16,128]{2,1,0:T(8,128)(2,1)S(1)} %sum.4), channel_id=1, replica_groups=mesh['pix'=16,'frm'=2] {'frm','pix'}, dimensions={0} | all-to-all | bytes 262144 | tf_op jit(solution)/shard_map/all_to_all | solution.py:328
  78.2 1.2 %step.5 = bf16[32,16,128]{2,1,0:T(8,128)(2,1)S(1)} custom-call(bf16[32,16,128]{2,1,0:T(8,128)(2,1)S(1)} %all_to_all.45.span_ref, f32[1,256]{1,0:T(1,128)S(1)} %get-tuple-element.12.weight_ref, bf16[512,1024]{1,0:T(8,128)(2,1)S(1)} %copy-done.1, bf16[256,1024]{1,0:T(8,128)(2,1)S(1)} %collective-permute-done.refs_0_.refs_1_), custom_call_target="tpu_custom_call" | custom-call | tf_op jit(solution)/shard_map/step/pallas_call | solution.py:330
  79.4 9.9 %all_to_all.46.in_ref = bf16[32,16,128]{2,1,0:T(8,128)(2,1)S(1)} all-to-all(bf16[32,16,128]{2,1,0:T(8,128)(2,1)S(1)} %step.5), channel_id=1, replica_groups=mesh['pix'=16,'frm'=2] {'frm','pix'}, dimensions={0} | all-to-all | bytes 262144 | tf_op jit(solution)/shard_map/all_to_all | solution.py:314
  89.3 0.2 sum.5
  89.5 9.9 %all_to_all.47.span_ref = bf16[32,16,128]{2,1,0:T(8,128)(2,1)S(1)} all-to-all(bf16[32,16,128]{2,1,0:T(8,128)(2,1)S(1)} %sum.5), channel_id=1, replica_groups=mesh['pix'=16,'frm'=2] {'frm','pix'}, dimensions={0} | all-to-all | bytes 262144 | tf_op jit(solution)/shard_map/all_to_all | solution.py:328
  99.4 0.8 fit.1.own_ref
  100.3 0.1 collective-permute-start.2
  100.3 1.2 %collective-permute-done.2.other_ref = f32[32,256]{1,0:T(8,128)S(1)} collective-permute-done((f32[32,256]{1,0:T(8,128)S(1)}, f32[32,256]{1,0:T(8,128)S(1)}, u32[]{:S(2)}, u32[]{:S(2)}) %collective-permute-start.2) | collective-permute-done | bytes 32800 | tf_op jit(solution)/shard_map/ppermute | solution.py:271
  101.5 0.6 place.1
  (1 shorter events, 0.0 us)
Async XLA Ops:
  0.0 1.2 %copy-start = (bf16[512,1024]{1,0:T(8,128)(2,1)S(1)}, bf16[512,1024]{1,0:T(8,128)(2,1)}, u32[]{:S(2)}) copy-start(bf16[512,1024]{1,0:T(8,128)(2,1)} %refs_0_.7) | copy-start | bytes 3145732
  1.2 0.9 copy-start.2
  1.2 1.6 %copy-start.1 = (bf16[512,1024]{1,0:T(8,128)(2,1)S(1)}, bf16[512,1024]{1,0:T(8,128)(2,1)}, u32[]{:S(2)}) copy-start(bf16[512,1024]{1,0:T(8,128)(2,1)} %refs_0_.7) | copy-start | bytes 3145732
  1.3 0.9 copy-start.5
  1.3 2.5 %collective-permute-start = (bf16[256,1024]{1,0:T(8,128)(2,1)S(1)}, bf16[256,1024]{1,0:T(8,128)(2,1)S(1)}, u32[]{:S(2)}, u32[]{:S(2)}) collective-permute-start(bf16[256,1024]{1,0:T(8,128)(2,1)S(1)} %pack.1), channel_id=1, source_target_pairs={{0,1},{1,0},{2,3},{3,2},{4,5},{5,4},{6,7},{7,6},{8,9},{9,8},{10,11... | collective-permute-start | bytes 1572872 | tf_op jit(solution)/shard_map/ppermute | solution.py:271
  2.2 0.8 copy-start.3
  2.2 0.8 copy-start.4
  2.3 1.4 %collective-permute-start.1 = (bf16[32,1024]{1,0:T(8,128)(2,1)S(1)}, bf16[32,1024]{1,0:T(8,128)(2,1)S(1)}, u32[]{:S(2)}, u32[]{:S(2)}) collective-permute-start(bf16[32,1024]{1,0:T(8,128)(2,1)S(1)} %pick.1), channel_id=1, source_target_pairs={{0,1},{1,0},{2,3},{3,2},{4,5},{5,4},{6,7},{7,6},{8,9},{9,8},{10,11... | collective-permute-start | bytes 196616 | tf_op jit(solution)/shard_map/ppermute | solution.py:271
  100.3 1.3 %collective-permute-start.2 = (f32[32,256]{1,0:T(8,128)S(1)}, f32[32,256]{1,0:T(8,128)S(1)}, u32[]{:S(2)}, u32[]{:S(2)}) collective-permute-start(f32[32,256]{1,0:T(8,128)S(1)} %fit.1.own_ref), channel_id=1, source_target_pairs={{0,1},{1,0},{2,3},{3,2},{4,5},{5,4},{6,7},{7,6},{8,9},{9,8},{10,11... | collective-permute-start | bytes 98312 | tf_op jit(solution)/shard_map/ppermute | solution.py:271

commit v7 on v6

--- a/solution.py
+++ b/solution.py
@@ -127,14 +127,15 @@
     label = entry(ann_ref, frm * chunk // block)
     raw_ref[...] = dot_rows(start_ref[label], mine(own_ref, chunk))
     npix = mark_ref.shape[0] // others
-    place = lax.broadcasted_iota(jnp.int32, mark_ref.shape, 0)
+    place = lax.broadcasted_iota(jnp.int32, (mark_ref.shape[0], LANES), 0)
     blocks = place % npix * ann_ref.shape[1] + place // npix * chunk // block
-    marks = jnp.full(mark_ref.shape, -1, jnp.int32)
+    marks = jnp.full(place.shape, -1, jnp.int32)
     for a in range(listed_ref.shape[0]):
         for at in range(listed_ref.shape[1]):
             marks = jnp.where(blocks == listed_ref[a : a + 1, at : at + 1], a, marks)
-    mark_ref[...] = marks
-    listed = mark_ref[pl.ds(frm * npix + pix, 1), :] >= 0
+    for j in range(mark_ref.shape[0]):
+        mark_ref[j] = jnp.broadcast_to(marks[j : j + 1, :], mark_ref.shape[1:])
+    listed = mark_ref[frm * npix + pix][:1, :] >= 0
     kept = keep_ref[pl.ds(frm, 1), :]
     weight_ref[...] = jnp.where((kept == 1) & listed[:, :1], 1.0, 0.0)
     say_ref[...] = jnp.where(listed, 0, label).astype(jnp.float32)
@@ -207,14 +208,15 @@
 def add_and_give(annuli, in_ref, mark_ref, give_ref, out_ref):
     parts, rows = out_ref.shape[:2]
 
+    def over(ref, j):
+        return jnp.concatenate([ref[j]] * (rows // ref.shape[1]), axis=0)
+
     def add(j, sums):
-        part = in_ref[j].astype(jnp.float32)
-        mark = mark_ref[pl.ds(j, 1), :]
+        part, mark = in_ref[j].astype(jnp.float32), over(mark_ref, j)
         return tuple(s + jnp.where(mark == a, part, 0.0) for a, s in enumerate(sums))
 
     def give(j, sums):
-        mark = give_ref[pl.ds(j, 1), :]
-        total = sums[0]
+        mark, total = over(give_ref, j), sums[0]
         for a in range(1, annuli):
             total = jnp.where(mark == a, sums[a], total)
         out_ref[j] = total.astype(out_ref.dtype)
@@ -233,9 +235,8 @@
 
 def first_sum_kernel(annuli, in_ref, mark_ref, out_ref, give_ref):
     for j in range(in_ref.shape[0]):
-        label = mark_ref[j : j + 1, :]
-        said = in_ref[j, :1, :].astype(jnp.int32)
-        give_ref[j : j + 1, :] = jnp.where(label < 0, said, label)
+        label, said = mark_ref[j], in_ref[j, :1, :].astype(jnp.int32)
+        give_ref[j] = jnp.where(label < 0, jnp.broadcast_to(said, label.shape), label)
     add_and_give(annuli, in_ref, mark_ref, give_ref, out_ref)
 
 
@@ -255,6 +256,7 @@
     vmem = pl.BlockSpec(memory_space=pltpu.VMEM)
     hbm = pl.BlockSpec(memory_space=pltpu.HBM)
     shape = jax.ShapeDtypeStruct
+    table = shape((parts, min(rows, 8), LANES), jnp.int32)
 
     def call(kernel, out, ins, outs, name, scratch=(), mib=32):
         return pl.pallas_call(
@@ -293,7 +295,7 @@
             shape((comps, chunk), jnp.float32),
             shape((1, chunk), jnp.float32),
             shape((1, LANES), jnp.float32),
-            shape((parts, LANES), jnp.int32),
+            table,
         ),
         [vmem] * 5,
         (vmem, vmem, vmem, vmem),
@@ -316,7 +318,7 @@
         if step == 0:
             total, give = call(
                 functools.partial(first_sum_kernel, annuli),
-                (total, shape((parts, LANES), jnp.int32)),
+                (total, table),
                 [vmem, vmem],
                 (vmem, vmem),
                 "first_sum",

time: 103 us -> 102 us (level)
  no operation moved by 1% of the time
where the time goes in v7:
time: 102 us
  blocking collectives  90.3 us (89%)
  Pallas kernels  7.01 us (7%)
  local copies, waits for them, and re-layouts  1.71 us (2%)
  waiting for transfers between devices  1.67 us (2%)
  starting transfers between devices  1.11 us (1%)
    all_to_all x4, blocking collectives, shards(): taken = lax.all_to_all(sent, BOTH, 0, 0, tiled=True)  47.7 us
    all_to_all x4, blocking collectives, shards(): span = lax.all_to_all(total, BOTH, 0, 0, tiled=True)  42.6 us
    pallas_call x4, Pallas kernels, shards(): call(functools.partial(step_kernel, last, nfrm), shape((comps, chunk), jn...  4.57 us
  transfers between devices with their start and end apart: 3, of which 2 were waited for; matrix products, arithmetic and copies ran while one was open for 0% of the time, Pallas kernels for 0%

profile of v7, /device:TPU:0, one launch (start us, length us, event | category | flops | bytes accessed | tf_op | source)
XLA Modules:
  0.0 101.8 jit_solution(18265861558825378238)
XLA Ops:
  0.0 0.0 copy-start
  0.0 1.2 %copy-done = bf16[512,1024]{1,0:T(8,128)(2,1)S(1)} copy-done((bf16[512,1024]{1,0:T(8,128)(2,1)S(1)}, bf16[512,1024]{1,0:T(8,128)(2,1)}, u32[]{:S(2)}) %copy-start) | copy-done | bytes 1048600
  1.2 0.0 copy-start.2
  1.2 0.0 copy-start.1
  1.3 0.0 copy-start.5
  1.3 0.5 collective-permute-start
  1.8 0.4 copy-done.2
  2.2 0.0 copy-done.5
  2.2 0.0 copy-start.3
  2.2 0.0 copy-start.4
  2.2 0.1 pick.1
  2.3 0.5 collective-permute-start.1
  2.8 0.0 copy-done.1
  2.8 0.1 copy-done.3
  2.9 0.0 copy-done.4
  3.0 0.3 own_part.1
  3.3 0.5 collective-permute-done.1.refs_1_
  3.7 0.0 collective-permute-done.refs_0_.refs_1_
  3.8 0.7 first_span.1
  4.5 18.2 %all_to_all.40.in_ref = f32[32,16,128]{2,1,0:T(8,128)S(1)} all-to-all(f32[32,16,128]{2,1,0:T(8,128)S(1)} %first_span.1), channel_id=1, replica_groups=mesh['pix'=16,'frm'=2] {'frm','pix'}, dimensions={0} | all-to-all | bytes 524288 | tf_op jit(solution)/shard_map/all_to_all | solution.py:316
  22.7 0.1 first_sum.1
  22.9 12.9 %all_to_all.41.span_ref = f32[32,16,128]{2,1,0:T(8,128)S(1)} all-to-all(f32[32,16,128]{2,1,0:T(8,128)S(1)} %get-tuple-element.15), channel_id=1, replica_groups=mesh['pix'=16,'frm'=2] {'frm','pix'}, dimensions={0} | all-to-all | bytes 524288 | tf_op jit(solution)/shard_map/all_to_all | solution.py:330
  35.8 1.4 %step.3 = bf16[32,16,128]{2,1,0:T(8,128)(2,1)S(1)} custom-call(f32[32,16,128]{2,1,0:T(8,128)S(1)} %all_to_all.41.span_ref, f32[1,256]{1,0:T(1,128)S(1)} %get-tuple-element.12.weight_ref, bf16[512,1024]{1,0:T(8,128)(2,1)S(1)} %copy-done.1, bf16[256,1024]{1,0:T(8,128)(2,1)S(1)} %collective-permute-done.refs_0_.refs_1_), custom_call_target="tpu_custom_call" | custom-call | tf_op jit(solution)/shard_map/step/pallas_call | solution.py:332
  37.2 9.6 %all_to_all.42.in_ref = bf16[32,16,128]{2,1,0:T(8,128)(2,1)S(1)} all-to-all(bf16[32,16,128]{2,1,0:T(8,128)(2,1)S(1)} %step.3), channel_id=1, replica_groups=mesh['pix'=16,'frm'=2] {'frm','pix'}, dimensions={0} | all-to-all | bytes 262144 | tf_op jit(solution)/shard_map/all_to_all | solution.py:316
  46.8 0.1 sum.3
  47.0 9.8 %all_to_all.43.span_ref = bf16[32,16,128]{2,1,0:T(8,128)(2,1)S(1)} all-to-all(bf16[32,16,128]{2,1,0:T(8,128)(2,1)S(1)} %sum.3), channel_id=1, replica_groups=mesh['pix'=16,'frm'=2] {'frm','pix'}, dimensions={0} | all-to-all | bytes 262144 | tf_op jit(solution)/shard_map/all_to_all | solution.py:330
  56.8 1.2 %step.4 = bf16[32,16,128]{2,1,0:T(8,128)(2,1)S(1)} custom-call(bf16[32,16,128]{2,1,0:T(8,128)(2,1)S(1)} %all_to_all.43.span_ref, f32[1,256]{1,0:T(1,128)S(1)} %get-tuple-element.12.weight_ref, bf16[512,1024]{1,0:T(8,128)(2,1)S(1)} %copy-done.1, bf16[256,1024]{1,0:T(8,128)(2,1)S(1)} %collective-permute-done.refs_0_.refs_1_), custom_call_target="tpu_custom_call" | custom-call | tf_op jit(solution)/shard_map/step/pallas_call | solution.py:332
  57.9 9.9 %all_to_all.44.in_ref = bf16[32,16,128]{2,1,0:T(8,128)(2,1)S(1)} all-to-all(bf16[32,16,128]{2,1,0:T(8,128)(2,1)S(1)} %step.4), channel_id=1, replica_groups=mesh['pix'=16,'frm'=2] {'frm','pix'}, dimensions={0} | all-to-all | bytes 262144 | tf_op jit(solution)/shard_map/all_to_all | solution.py:316
  67.9 0.1 sum.4
  68.0 9.9 %all_to_all.45.span_ref = bf16[32,16,128]{2,1,0:T(8,128)(2,1)S(1)} all-to-all(bf16[32,16,128]{2,1,0:T(8,128)(2,1)S(1)} %sum.4), channel_id=1, replica_groups=mesh['pix'=16,'frm'=2] {'frm','pix'}, dimensions={0} | all-to-all | bytes 262144 | tf_op jit(solution)/shard_map/all_to_all | solution.py:330
  77.9 1.2 %step.5 = bf16[32,16,128]{2,1,0:T(8,128)(2,1)S(1)} custom-call(bf16[32,16,128]{2,1,0:T(8,128)(2,1)S(1)} %all_to_all.45.span_ref, f32[1,256]{1,0:T(1,128)S(1)} %get-tuple-element.12.weight_ref, bf16[512,1024]{1,0:T(8,128)(2,1)S(1)} %copy-done.1, bf16[256,1024]{1,0:T(8,128)(2,1)S(1)} %collective-permute-done.refs_0_.refs_1_), custom_call_target="tpu_custom_call" | custom-call | tf_op jit(solution)/shard_map/step/pallas_call | solution.py:332
  79.1 9.9 %all_to_all.46.in_ref = bf16[32,16,128]{2,1,0:T(8,128)(2,1)S(1)} all-to-all(bf16[32,16,128]{2,1,0:T(8,128)(2,1)S(1)} %step.5), channel_id=1, replica_groups=mesh['pix'=16,'frm'=2] {'frm','pix'}, dimensions={0} | all-to-all | bytes 262144 | tf_op jit(solution)/shard_map/all_to_all | solution.py:316
  89.0 0.1 sum.5
  89.2 9.9 %all_to_all.47.span_ref = bf16[32,16,128]{2,1,0:T(8,128)(2,1)S(1)} all-to-all(bf16[32,16,128]{2,1,0:T(8,128)(2,1)S(1)} %sum.5), channel_id=1, replica_groups=mesh['pix'=16,'frm'=2] {'frm','pix'}, dimensions={0} | all-to-all | bytes 262144 | tf_op jit(solution)/shard_map/all_to_all | solution.py:330
  99.1 0.8 fit.1.own_ref
  99.9 0.1 collective-permute-start.2
  100.0 1.2 %collective-permute-done.2.other_ref = f32[32,256]{1,0:T(8,128)S(1)} collective-permute-done((f32[32,256]{1,0:T(8,128)S(1)}, f32[32,256]{1,0:T(8,128)S(1)}, u32[]{:S(2)}, u32[]{:S(2)}) %collective-permute-start.2) | collective-permute-done | bytes 32800 | tf_op jit(solution)/shard_map/ppermute | solution.py:273
  101.2 0.6 place.1
  (1 shorter events, 0.0 us)
Async XLA Ops:
  0.0 1.2 %copy-start = (bf16[512,1024]{1,0:T(8,128)(2,1)S(1)}, bf16[512,1024]{1,0:T(8,128)(2,1)}, u32[]{:S(2)}) copy-start(bf16[512,1024]{1,0:T(8,128)(2,1)} %refs_0_.7) | copy-start | bytes 3145732
  1.2 0.9 copy-start.2
  1.2 1.6 %copy-start.1 = (bf16[512,1024]{1,0:T(8,128)(2,1)S(1)}, bf16[512,1024]{1,0:T(8,128)(2,1)}, u32[]{:S(2)}) copy-start(bf16[512,1024]{1,0:T(8,128)(2,1)} %refs_0_.7) | copy-start | bytes 3145732
  1.3 0.9 copy-start.5
  1.3 2.5 %collective-permute-start = (bf16[256,1024]{1,0:T(8,128)(2,1)S(1)}, bf16[256,1024]{1,0:T(8,128)(2,1)S(1)}, u32[]{:S(2)}, u32[]{:S(2)}) collective-permute-start(bf16[256,1024]{1,0:T(8,128)(2,1)S(1)} %pack.1), channel_id=1, source_target_pairs={{0,1},{1,0},{2,3},{3,2},{4,5},{5,4},{6,7},{7,6},{8,9},{9,8},{10,11... | collective-permute-start | bytes 1572872 | tf_op jit(solution)/shard_map/ppermute | solution.py:273
  2.2 0.8 copy-start.3
  2.2 0.8 copy-start.4
  2.3 1.4 %collective-permute-start.1 = (bf16[32,1024]{1,0:T(8,128)(2,1)S(1)}, bf16[32,1024]{1,0:T(8,128)(2,1)S(1)}, u32[]{:S(2)}, u32[]{:S(2)}) collective-permute-start(bf16[32,1024]{1,0:T(8,128)(2,1)S(1)} %pick.1), channel_id=1, source_target_pairs={{0,1},{1,0},{2,3},{3,2},{4,5},{5,4},{6,7},{7,6},{8,9},{9,8},{10,11... | collective-permute-start | bytes 196616 | tf_op jit(solution)/shard_map/ppermute | solution.py:273
  99.9 1.3 %collective-permute-start.2 = (f32[32,256]{1,0:T(8,128)S(1)}, f32[32,256]{1,0:T(8,128)S(1)}, u32[]{:S(2)}, u32[]{:S(2)}) collective-permute-start(f32[32,256]{1,0:T(8,128)S(1)} %fit.1.own_ref), channel_id=1, source_target_pairs={{0,1},{1,0},{2,3},{3,2},{4,5},{5,4},{6,7},{7,6},{8,9},{9,8},{10,11... | collective-permute-start | bytes 98312 | tf_op jit(solution)/shard_map/ppermute | solution.py:273
